TPU v7x, 32 devices: a whole 2x2x4 slice. The times are simulated.
32 devices in a mesh: src: 8 (over z, y), rcv: 4 (over x, core).
Axes of the slice: x: 2, y: 2, z: 4, core: 2. Of those that a mesh axis runs over, the one named last changes fastest.
Arguments:
- src_coords: float32 [3, 16], P(None, 'src'), may hold values from -1 to 1
- rcv_coords: float32 [3, 16, 2048], P(None, 'src', 'rcv'), may hold values from -1 to 1
- velocity: float32 [16, 2048], P('src', 'rcv'), may hold values from 0.5 to 2
- pair_mask: int32 [16, 2048], P('src', 'rcv'), may hold values from 0 to 1, as said below
- near_flag: int32 [16, 2048], P('src', 'rcv'), may hold values 0 or 1
- block_params: float32 [2048, 512], P(('src', 'rcv')), may hold values from -0.25 to 0.25
- edge_params: float32 [6144], P(('src', 'rcv'))
- block_moment: float32 [2048, 512], P(('src', 'rcv')), may hold values from -0.0007324219 to 0.0007324219
- edge_moment: float32 [6144], P(('src', 'rcv')), may hold values from -0.001953125 to 0.001953125
- block_second: float32 [2048, 512], P(('src', 'rcv')), may hold values from 2.3702973e-09 to 9.481189e-09
- edge_second: float32 [6144], P(('src', 'rcv')), may hold values from 2.1332676e-08 to 8.5330704e-08
Outputs:
- grad_norm: float32 [], replicated
- new_blocks: float32 [2048, 512], P(('src', 'rcv'))
- new_edges: float32 [6144], P(('src', 'rcv'))
- moment_blocks: float32 [2048, 512], P(('src', 'rcv'))
- moment_edges: float32 [6144], P(('src', 'rcv'))
- second_blocks: float32 [2048, 512], P(('src', 'rcv'))
- second_edges: float32 [6144], P(('src', 'rcv'))
- low_blocks: bfloat16 [2048, 512], P(('src', 'rcv'))
- low_edges: bfloat16 [6144], P(('src', 'rcv'))
Inputs may be any that keep to these rules, and one draw needn't show every extreme that they name: `pair_mask`: 1 marks a pair that enters the loss.
All inputs are finite; a program needn't handle non-finite values. No bound on the sum of `near_flag` on one device may be relied on, other than what follows from the above.
Results may differ from a plain program's by a relative error of at most 0.001.
Values sent between devices are 32-bit elements; how exact they have to be, the bound alone decides.
No kernel may reach another device: no remote copies, remote signals or barrier semaphores. Data moves between devices by JAX's collectives and lax.ppermute only.
A program may use at most 320 MiB of HBM per device.

v0:
```python
import jax
import jax.numpy as jnp
from jax import lax
from jax.sharding import PartitionSpec as P

ADAM_STEP = 5


clip_limit = 0.05
beta_one = 0.5
beta_two = 0.5
adam_eps = 1e-08
decay_rate = 0.01
block_rate = 0.02
edge_rate = 0.1


def matmul(left, right):
    return jnp.dot(left, right, precision=lax.Precision.HIGHEST)


def elu_slope(values):
    return jnp.where(values > 0, 1.0, jnp.exp(jnp.minimum(values, 0.0)))


def pair_loss(block_params, edge_params, sources, points_raw, velocity, live_pair, near_pair):
    feat_width = block_params.shape[1]
    edge_table = edge_params.reshape(12, feat_width)
    points = jnp.where(near_pair[None] == 1, sources + 0.1 * points_raw, points_raw)
    inputs = jnp.concatenate([sources, points], 0)
    hidden = matmul(inputs.T, edge_table[:6]) + edge_table[6]
    pair_total = hidden.shape[0]
    tangent = jnp.broadcast_to(edge_table[3:6][:, None, :], (3, pair_total, feat_width))
    stream = jnp.concatenate([hidden[None], tangent], 0)
    for layer_idx in range(2):
        result = stream
        for half_idx in range(2):
            which = 2 * layer_idx + half_idx
            matrix = block_params[which * feat_width : (which + 1) * feat_width]
            mapped = matmul(result.reshape(-1, feat_width), matrix).reshape(
                4, pair_total, feat_width
            )
            preact = mapped[0] + edge_table[7 + which]
            result = jnp.concatenate(
                [jax.nn.elu(preact)[None], elu_slope(preact)[None] * mapped[1:]], 0
            )
        stream = stream + result
    output = matmul(stream.reshape(-1, feat_width), edge_table[11]).reshape(4, pair_total)
    net_out = output[0]
    net_slope = output[1:]
    travel_ratio = jnp.sqrt(net_out * net_out + 1.0)
    ratio_slope = (net_out / travel_ratio)[None] * net_slope
    offset_vec = points - sources
    distance = jnp.sqrt(jnp.sum(offset_vec * offset_vec, 0) + 0.01)
    time_grad = travel_ratio[None] * offset_vec / distance[None] + distance[None] * ratio_slope
    grad_size = jnp.sqrt(jnp.sum(time_grad * time_grad, 0) + 0.01)
    misfit = velocity * grad_size - 1.0
    return jnp.sum(live_pair * misfit * misfit)


def adamw(weights, grads, first, second, rate):
    first_new = beta_one * first + (1.0 - beta_one) * grads
    second_new = beta_two * second + (1.0 - beta_two) * grads * grads
    first_hat = first_new / (1.0 - beta_one**ADAM_STEP)
    second_hat = second_new / (1.0 - beta_two**ADAM_STEP)
    weights_new = weights - rate * (
        first_hat / (jnp.sqrt(second_hat) + adam_eps) + decay_rate * weights
    )
    return (weights_new, first_new, second_new)


def local(
    src_coords,
    rcv_coords,
    velocity,
    pair_mask,
    near_flag,
    block_params,
    edge_params,
    block_moment,
    edge_moment,
    block_second,
    edge_second,
):
    live_local = pair_mask.astype(jnp.float32)
    count_local = jnp.sum(live_local)
    count_total = lax.psum(count_local, ("src", "rcv"))
    full_blocks, full_edges = (
        lax.all_gather(block_params, ("src", "rcv"), axis=0, tiled=True),
        lax.all_gather(edge_params, ("src", "rcv"), axis=0, tiled=True),
    )
    sources = jnp.broadcast_to(src_coords[:, :, None], rcv_coords.shape).reshape(3, -1)
    points_raw = rcv_coords.reshape(3, -1)

    def local_loss(bparams, eparams):
        return pair_loss(
            bparams,
            eparams,
            sources,
            points_raw,
            velocity.reshape(-1),
            live_local.reshape(-1),
            near_flag.reshape(-1),
        )

    value_local, pullback = jax.vjp(local_loss, full_blocks, full_edges)
    grad_b, grad_e = pullback(jnp.float32(1.0))
    summed_b, summed_e = (
        lax.psum_scatter(grad_b, ("src", "rcv"), scatter_dimension=0, tiled=True),
        lax.psum_scatter(grad_e, ("src", "rcv"), scatter_dimension=0, tiled=True),
    )
    local_sq = jnp.sum(summed_b * summed_b) + jnp.sum(summed_e * summed_e)
    total_sq = lax.psum(local_sq, ("src", "rcv"))
    count_all = jnp.maximum(count_total, 1.0)
    grad_norm = jnp.sqrt(total_sq) / count_all
    clip_factor = jnp.minimum(1.0, clip_limit / (grad_norm + 1e-06))
    grads_b = summed_b * clip_factor / count_all
    grads_e = summed_e * clip_factor / count_all
    new_blocks, moment_blocks, second_blocks = adamw(
        block_params, grads_b, block_moment, block_second, block_rate
    )
    new_edges, moment_edges, second_edges = adamw(
        edge_params, grads_e, edge_moment, edge_second, edge_rate
    )
    return (
        grad_norm,
        new_blocks,
        new_edges,
        moment_blocks,
        moment_edges,
        second_blocks,
        second_edges,
        new_blocks.astype(jnp.bfloat16),
        new_edges.astype(jnp.bfloat16),
    )


def solution(mesh):
    placed = (
        P(None, "src"),
        P(None, "src", "rcv"),
        P("src", "rcv"),
        P("src", "rcv"),
        P("src", "rcv"),
        P(("src", "rcv"), None),
        P(("src", "rcv")),
        P(("src", "rcv"), None),
        P(("src", "rcv")),
        P(("src", "rcv"), None),
        P(("src", "rcv")),
    )
    return jax.shard_map(
        local,
        mesh=mesh,
        in_specs=placed,
        out_specs=(
            P(),
            P(("src", "rcv"), None),
            P(("src", "rcv")),
            P(("src", "rcv"), None),
            P(("src", "rcv")),
            P(("src", "rcv"), None),
            P(("src", "rcv")),
            P(("src", "rcv"), None),
            P(("src", "rcv")),
        ),
        check_vma=False,
    )
```

profile of v0, /device:TPU:0, one launch (start us, length us, event | category | flops | bytes accessed | tf_op | source)
XLA Modules:
  0.0 620.7 jit_solution(14621120882059377300)
XLA Ops:
  8.9 42.3 %all-reduce.22 = f32[6144]{0:T(1024)S(1)} all-reduce(f32[6144]{0:T(1024)S(1)} %dynamic-update-slice), channel_id=1, replica_groups=mesh['src'=8,'rcv'=4] {'src','rcv'}, use_global_device_ids=true, to_apply=%add.22 | all-reduce | flops 6144 | bytes 49152
  54.3 1.3 convert_reduce_fusion
  56.3 1.9 add_bitcast_fusion
  59.6 2.6 copy-done.8
  62.2 4.3 pad_maximum_fusion
  66.5 9.9 %all-gather.2.cloned.1.call-done = f32[2048,512]{1,0:T(8,128)} async-done(((f32[64,512]{1,0:T(8,128)}), f32[2048,512]{1,0:T(8,128)}) %all-gather.2.cloned.1.call-update) | async-done | bytes 4194320 | tf_op jit(solution)/shard_map/all_gather | solution.py:89
  76.4 16.4 %fusion.45 = f32[4096,512]{1,0:T(8,128)S(1)} fusion(f32[4096,512]{1,0:T(8,128)} %bitcast.116, f32[2048,512]{1,0:T(8,128)} %all-gather.2.cloned.1.call-done), kind=kOutput, calls=%fused_computation.91 | convolution fusion | flops 12884901888 | bytes 17825792 | tf_op jit(solution)/shard_map/jvp()/dot_general | solution.py:19
  93.6 2.5 copy-done.9
  96.1 2.5 select_bitcast_fusion.3
  99.9 4.3 pad_maximum_fusion.1
  105.0 14.6 %fusion.42 = f32[4096,512]{1,0:T(8,128)S(1)} fusion(f32[4096,512]{1,0:T(8,128)S(1)} %bitcast.138, f32[2048,512]{1,0:T(8,128)S(1)} %copy-done.30), kind=kOutput, calls=%fused_computation.88 | convolution fusion | flops 12884901888 | bytes 17825792 | tf_op jit(solution)/shard_map/jvp()/dot_general | solution.py:19
  120.4 2.5 copy-done.1
  123.0 1.1 select_bitcast_fusion.2
  124.1 1.1 broadcast_multiply_fusion.5
  126.2 2.1 copy-done.2
  128.2 4.2 pad_maximum_fusion.2
  132.4 11.6 %bitcast_add_fusion.1 = f32[4096,512]{1,0:T(8,128)} fusion(f32[4,1024,512]{2,1,0:T(8,128)} %pad_maximum_fusion.2, f32[4,1024,512]{2,1,0:T(8,128)} %pad_maximum_fusion), kind=kLoop, calls=%fused_computation.6 | loop fusion | flops 2097152 | bytes 25165824 | tf_op jit(solution)/shard_map/jvp()/add | solution.py:47
  144.1 16.0 %fusion.38 = f32[4096,512]{1,0:T(8,128)S(1)} fusion(f32[4096,512]{1,0:T(8,128)} %bitcast_add_fusion.1, f32[2048,512]{1,0:T(8,128)S(1)} %copy-done.30), kind=kOutput, calls=%fused_computation.84 | convolution fusion | flops 12884901888 | bytes 17825792 | tf_op jit(solution)/shard_map/jvp()/dot_general | solution.py:19
  160.8 2.6 copy-done.10
  163.4 1.1 select_bitcast_fusion.1
  164.5 1.1 broadcast_multiply_fusion.4
  167.6 1.6 copy-done.15
  169.2 15.3 %fusion.35 = f32[4096,512]{1,0:T(8,128)S(1)} fusion(f32[4096,512]{1,0:T(8,128)S(1)} %bitcast.139, f32[2048,512]{1,0:T(8,128)} %all-gather.2.cloned.1.call-done), kind=kOutput, calls=%fused_computation.81 | convolution fusion | flops 12884901888 | bytes 17825792 | tf_op jit(solution)/shard_map/jvp()/dot_general | solution.py:19
  185.3 2.5 copy-done.11
  187.8 1.1 select_bitcast_fusion
  188.9 1.1 broadcast_multiply_fusion.2
  191.0 2.1 copy-done.3
  193.2 4.2 pad_maximum_fusion.4
  197.4 11.2 %bitcast_add_fusion = f32[4096,512]{1,0:T(8,128)} fusion(f32[4096,512]{1,0:T(8,128)} %bitcast_add_fusion.1, f32[4,1024,512]{2,1,0:T(8,128)} %pad_maximum_fusion.4), kind=kLoop, calls=%fused_computation.5 | loop fusion | flops 2097152 | bytes 25165824 | tf_op jit(solution)/shard_map/jvp()/add | solution.py:47
  208.6 9.4 %fusion.72 = f32[1,4096]{1,0:T(1,128)S(1)} fusion(f32[4096,512]{1,0:T(8,128)} %bitcast_add_fusion, f32[512,1]{0,1:T(1,128)S(1)} %bitcast.167), kind=kOutput, calls=%fused_computation.146 | convolution fusion | flops 25165824 | bytes 8407040 | tf_op jit(solution)/shard_map/jvp()/dot_general | solution.py:19
  218.3 1.1 broadcast_multiply_fusion
  219.4 3.3 split.49
  222.8 2.2 copy-done
  225.0 9.3 %broadcast_multiply_fusion.1 = (f32[3,1024,512]{2,1,0:T(8,128)}, f32[1024,512]{1,0:T(8,128)}) fusion(f32[3,1024,512]{2,1,0:T(8,128)} %bitcast.144, f32[1024,512]{1,0:T(8,128)} %copy-done.29, f32[3,1024,512]{2,1,0:T(8,128)S(1)} %bitcast.135), kind=kLoop, calls=%fused_computation.27 | loop fusion | flops 4194304 | bytes 23068672 | tf_op jit(solution)/shard_map/transpose(jvp())/mul | solution.py:45
  234.2 4.5 fusion.68
  238.8 3.9 pad_add_fusion.3
  242.8 17.0 %convolution_bitcast_fusion.1 = f32[512,512]{1,0:T(8,128)} fusion(f32[1,1024,512]{2,1,0:T(8,128)S(1)} %bitcast.154, f32[3,1024,512]{2,1,0:T(8,128)} %get-tuple-element.44, f32[3,1024,512]{2,1,0:T(8,128)S(1)} %bitcast.143, f32[1,1024,512]{2,1,0:T(8,128)S(1)} %copy-done.34), kind=kOutput, calls=%fused_computation.75 | convolution fusion | flops 12889096192 | bytes 17825792 | tf_op jit(solution)/shard_map/transpose(jvp())/dot_general | solution.py:19
  259.8 16.3 %fusion.33 = f32[4096,512]{1,0:T(8,128)S(1)} fusion(f32[4096,512]{1,0:T(8,128)S(1)} %bitcast.136, f32[2048,512]{1,0:T(8,128)} %all-gather.2.cloned.1.call-done), kind=kOutput, calls=%fused_computation.79 | convolution fusion | flops 12884901888 | bytes 17825792 | tf_op jit(solution)/shard_map/transpose(jvp())/dot_general | solution.py:19
  276.0 3.7 split.51
  279.8 2.4 copy-done.13
  282.2 11.3 %broadcast_multiply_fusion.3 = (f32[3,1024,512]{2,1,0:T(8,128)}, f32[1024,512]{1,0:T(8,128)}) fusion(f32[3,1024,512]{2,1,0:T(8,128)} %bitcast.145, f32[1024,512]{1,0:T(8,128)} %copy-done.28, f32[3,1024,512]{2,1,0:T(8,128)} %bitcast.131), kind=kLoop, calls=%fused_computation.29 | loop fusion | flops 4194304 | bytes 23068672 | tf_op jit(solution)/shard_map/transpose(jvp())/mul | solution.py:45
  293.5 5.8 fusion.69
  299.4 18.1 %fusion.25 = f32[512,512]{1,0:T(8,128)} fusion(f32[1,1024,512]{2,1,0:T(8,128)} %bitcast.151, f32[3,1024,512]{2,1,0:T(8,128)} %get-tuple-element.42, f32[3,1024,512]{2,1,0:T(8,128)} %copy-done.8, f32[1,1024,512]{2,1,0:T(8,128)} %copy-done.18, f32[3,1024,512]{2,1,0:T(8,128)S(1)} %bitcast.121, f32[1,1024,512]{2,1,0:T(8,128)} %copy-done.21), kind=kOutput, calls=%fused_computation.73 | convolution fusion | flops 12893290496 | bytes 26214400 | tf_op jit(solution)/shard_map/transpose(jvp())/dot_general | solution.py:19
  317.5 17.7 %fusion.9 = f32[4,1024,512]{2,1,0:T(8,128)} fusion(f32[4,1024,512]{2,1,0:T(8,128)S(1)} %bitcast.119, f32[1,1024,512]{2,1,0:T(8,128)} %bitcast.152, f32[3,1024,512]{2,1,0:T(8,128)S(1)} %bitcast.148, f32[2048,512]{1,0:T(8,128)} %all-gather.2.cloned.1.call-done), kind=kOutput, calls=%fused_computation.35 | convolution fusion | flops 12889096192 | bytes 26214400 | tf_op jit(solution)/shard_map/transpose(jvp())/dot_general | solution.py:19
  335.3 9.5 %slice_multiply_fusion = (f32[3,1024,512]{2,1,0:T(8,128)}, f32[1024,512]{1,0:T(8,128)S(1)}) fusion(f32[4,1024,512]{2,1,0:T(8,128)} %fusion.9, f32[1024,512]{1,0:T(8,128)S(1)} %copy-done.27, f32[3,1024,512]{2,1,0:T(8,128)} %bitcast.129), kind=kLoop, calls=%fused_computation.22 | loop fusion | flops 4194304 | bytes 23068672 | tf_op jit(solution)/shard_map/transpose(jvp())/mul | solution.py:45
  344.8 4.5 fusion.19
  349.3 3.9 pad_add_fusion.1
  353.3 16.9 %convolution_bitcast_fusion = f32[512,512]{1,0:T(8,128)} fusion(f32[1,1024,512]{2,1,0:T(8,128)S(1)} %fusion.19, f32[3,1024,512]{2,1,0:T(8,128)} %get-tuple-element.38, f32[3,1024,512]{2,1,0:T(8,128)S(1)} %bitcast.141, f32[1,1024,512]{2,1,0:T(8,128)S(1)} %copy-done.32), kind=kOutput, calls=%fused_computation.74 | convolution fusion | flops 12889096192 | bytes 17825792 | tf_op jit(solution)/shard_map/transpose(jvp())/dot_general | solution.py:19
  370.2 16.4 %fusion.40 = f32[4096,512]{1,0:T(8,128)S(1)} fusion(f32[4096,512]{1,0:T(8,128)S(1)} %bitcast.137, f32[2048,512]{1,0:T(8,128)} %all-gather.2.cloned.1.call-done), kind=kOutput, calls=%fused_computation.86 | convolution fusion | flops 12884901888 | bytes 17825792 | tf_op jit(solution)/shard_map/transpose(jvp())/dot_general | solution.py:19
  386.7 3.7 split.55
  390.4 1.4 copy-done.12
  391.9 9.4 %broadcast_multiply_fusion.6 = (f32[3,1024,512]{2,1,0:T(8,128)}, f32[1024,512]{1,0:T(8,128)}) fusion(f32[3,1024,512]{2,1,0:T(8,128)} %bitcast.146, f32[1024,512]{1,0:T(8,128)} %copy-done.25, f32[3,1024,512]{2,1,0:T(8,128)S(1)} %bitcast.127), kind=kLoop, calls=%fused_computation.32 | loop fusion | flops 4194304 | bytes 23068672 | tf_op jit(solution)/shard_map/transpose(jvp())/mul | solution.py:45
  401.3 6.3 %fusion.70 = (f32[512]{0:T(512)S(1)}, f32[1024,512]{1,0:T(8,128)S(1)}, f32[512]{0:T(512)S(1)}) fusion(f32[4096,512]{1,0:T(8,128)} %copy-done.12, f32[1024,512]{1,0:T(8,128)} %get-tuple-element.41, f32[512]{0:T(512)S(1)} %copy-done.42, f32[4096,512]{1,0:T(8,128)} %copy-done.9, f32[4,1024,512]{2,1,0:T(8,128)} %fusion.9, f32[1024,512]{1,0:T(8,128)} %copy-done.17, ...), kind=kLoop, calls=%fused_computation.144 | loop fusion | flops 18873344 | bytes 14688256 | tf_op jit(solution)/shard_map/transpose(jvp())/reduce_sum | solution.py:43
  407.6 1.3 copy-done.31
  408.9 17.0 %fusion.24 = f32[512,512]{1,0:T(8,128)S(1)} fusion(f32[1,1024,512]{2,1,0:T(8,128)S(1)} %bitcast.149, f32[3,1024,512]{2,1,0:T(8,128)S(1)} %copy-done.16, f32[3,1024,512]{2,1,0:T(8,128)} %copy-done.8, f32[1,1024,512]{2,1,0:T(8,128)S(1)} %copy-done.19), kind=kOutput, calls=%fused_computation.72 | convolution fusion | flops 12889096192 | bytes 17825792 | tf_op jit(solution)/shard_map/transpose(jvp())/dot_general | solution.py:19
  426.0 2.5 pad_add_fusion.8
  428.5 17.2 %fusion.8 = f32[4,1024,512]{2,1,0:T(8,128)S(1)} fusion(f32[4,1024,512]{2,1,0:T(8,128)} %fusion.9, f32[1,1024,512]{2,1,0:T(8,128)} %bitcast.150, f32[3,1024,512]{2,1,0:T(8,128)} %get-tuple-element.40, f32[2048,512]{1,0:T(8,128)} %all-gather.2.cloned.1.call-done), kind=kOutput, calls=%fused_computation.34 | convolution fusion | flops 12889096192 | bytes 26214400 | tf_op jit(solution)/shard_map/transpose(jvp())/dot_general | solution.py:19
  445.9 1.1 fusion.10
  448.7 7.8 %fusion.28 = f32[1,512]{1,0:T(1,128)S(1)} fusion(f32[3,1024,512]{2,1,0:T(8,128)} %copy-done.8, f32[1,1024,512]{2,1,0:T(8,128)S(1)} %copy-done.20, f32[4,1024,1]{1,0,2:T(4,128)S(1)} %get-tuple-element.53, f32[3,1024,512]{2,1,0:T(8,128)} %copy-done.3, f32[1,1024,512]{2,1,0:T(8,128)S(1)} %copy-done.24, f32[3,1024,512]{2,1,0:T(8,128)S(1)} %bitcast.123, ...), kind=kOutput, calls=%fused_computation.76 | convolution fusion | flops 35651584 | bytes 25184256 | tf_op jit(solution)/shard_map/transpose(jvp())/dot_general | solution.py:19
  456.6 38.6 %all-reduce.23 = f32[6144]{0:T(1024)S(1)} all-reduce(f32[6144]{0:T(1024)S(1)} %reshape.402), channel_id=3, replica_groups=mesh['src'=8,'rcv'=4] {'src','rcv'}, use_global_device_ids=true, to_apply=%region_16.17.clone | all-reduce | flops 6144 | bytes 49152
  495.8 72.6 %reduce-scatter.2.cloned.1.call-done = f32[64,512]{1,0:T(8,128)} async-done(((f32[2048,512]{1,0:T(8,128)}), f32[64,512]{1,0:T(8,128)}) %reduce-scatter.2.cloned.1.call-update) | async-done | bytes 131088 | tf_op jit(solution)/shard_map/reduce_scatter | solution.py:109
  568.5 1.5 multiply_reduce_fusion.4
  571.3 37.1 %all-reduce.24 = (f32[]{:T(128)}, f32[]{:T(128)}) all-reduce(f32[]{:T(128)S(6)} %add.205, f32[]{:T(128)} %get-tuple-element.57), channel_id=1, replica_groups=mesh['src'=8,'rcv'=4] {'src','rcv'}, use_global_device_ids=true, to_apply=%region_18.19 | all-reduce | flops 2 | bytes 16 | tf_op jit(solution)/shard_map/psum | solution.py:113
  610.6 1.7 fusion.66
  (164 shorter events, 19.6 us)
Async XLA Ops:
  7.2 69.2 %all-gather.2.cloned.1.call-start = ((), (), s32[]{:S(2)}) async-start(), calls=%async_computation.1 | async-start | bytes 4325376 | tf_op jit(solution)/shard_map/all_gather | solution.py:89
  7.9 560.6 %reduce-scatter.2.cloned.1.call-start = ((), (), s32[]{:S(2)}) async-start(), calls=%async_computation.2 | async-start | bytes 4325376 | tf_op jit(solution)/shard_map/reduce_scatter | solution.py:109
  56.3 37.3 %copy-start.41 = (f32[512]{0:T(512)}, f32[512]{0:T(512)S(1)}, u32[]{:S(2)}) copy-start(f32[512]{0:T(512)S(1)} %get-tuple-element.50) | copy-start | bytes 6148
  58.1 1.4 copy-start.18
  59.6 2.6 copy-start.8
  92.8 3.3 copy-start.9
  93.6 6.0 copy-start.4
  98.5 1.4 copy-start.25
  99.9 4.3 copy-start.14
  99.9 5.1 copy-start.30
  119.7 3.3 copy-start.1
  120.4 4.7 copy-start.5
  124.1 1.6 copy-start.26
  124.1 2.1 copy-start.21
  125.6 2.6 copy-start.2
  160.0 3.4 copy-start.10
  160.8 4.8 copy-start.6
  164.5 1.5 copy-start.28
  164.5 2.1 copy-start.33
  166.0 3.1 copy-start.15
  184.5 3.3 copy-start.11
  185.3 4.7 copy-start.7
  188.9 1.6 copy-start.29
  188.9 2.1 copy-start.23
  190.4 2.7 copy-start.3
  218.3 6.7 %slice-start.8 = ((s8[6291456]{0:T(1024)(128)(4,1)}), s8[4194304]{0:T(1024)(128)(4,1)S(1)}, s32[]{:S(2)}) async-start(s8[6291456]{0:T(1024)(128)(4,1)} %bitcast.133), calls=%async_computation.11 | async-start | bytes 8388608
  219.4 5.5 copy-start
  219.4 5.5 slice-start.9
  234.2 8.4 %slice-start.12 = ((s8[6291456]{0:T(1024)(128)(4,1)}), s8[4194304]{0:T(1024)(128)(4,1)S(1)}, s32[]{:S(2)}) async-start(s8[6291456]{0:T(1024)(128)(4,1)} %bitcast.142), calls=%async_computation.15 | async-start | bytes 8388608
  238.8 3.9 slice-start.13
  238.8 4.0 copy-start.34
  276.0 6.2 copy-start.13
  276.0 23.3 %slice-start.2 = ((s8[6291456]{0:T(1024)(128)(4,1)}), s8[4194304]{0:T(1024)(128)(4,1)S(1)}, s32[]{:S(2)}) async-start(s8[6291456]{0:T(1024)(128)(4,1)} %bitcast.120), calls=%async_computation.5 | async-start | bytes 8388608
  282.2 17.1 %slice-start.3 = ((s8[6291456]{0:T(1024)(128)(4,1)}), s8[2097152]{0:T(1024)(128)(4,1)S(1)}, s32[]{:S(2)}) async-start(s8[6291456]{0:T(1024)(128)(4,1)} %bitcast.120), calls=%async_computation.6 | async-start | bytes 4194304
  293.5 24.0 %slice-start = ((s8[8388608]{0:T(1024)(128)(4,1)}), s8[4194304]{0:T(1024)(128)(4,1)S(1)}, s32[]{:S(2)}) async-start(s8[8388608]{0:T(1024)(128)(4,1)} %bitcast.117), calls=%async_computation.3 | async-start | bytes 8388608
  293.5 24.0 %slice-start.14 = ((s8[6291456]{0:T(1024)(128)(4,1)}), s8[4194304]{0:T(1024)(128)(4,1)S(1)}, s32[]{:S(2)}) async-start(s8[6291456]{0:T(1024)(128)(4,1)} %bitcast.147), calls=%async_computation.17 | async-start | bytes 8388608
  299.4 18.1 %slice-start.1 = ((s8[8388608]{0:T(1024)(128)(4,1)}), s8[4194304]{0:T(1024)(128)(4,1)S(1)}, s32[]{:S(2)}) async-start(s8[8388608]{0:T(1024)(128)(4,1)} %bitcast.117), calls=%async_computation.4 | async-start | bytes 8388608
  299.4 18.1 %slice-start.15 = ((s8[6291456]{0:T(1024)(128)(4,1)}), s8[2097152]{0:T(1024)(128)(4,1)S(1)}, s32[]{:S(2)}) async-start(s8[6291456]{0:T(1024)(128)(4,1)} %bitcast.147), calls=%async_computation.18 | async-start | bytes 4194304
  317.5 17.8 %copy-start.27 = (f32[1024,512]{1,0:T(8,128)S(1)}, f32[1024,512]{1,0:T(8,128)}, u32[]{:S(2)}) copy-start(f32[1024,512]{1,0:T(8,128)} %copy-done.26) | copy-start | bytes 6291460
  344.8 4.5 copy-start.17
  344.8 8.4 %slice-start.10 = ((s8[6291456]{0:T(1024)(128)(4,1)}), s8[4194304]{0:T(1024)(128)(4,1)S(1)}, s32[]{:S(2)}) async-start(s8[6291456]{0:T(1024)(128)(4,1)} %bitcast.140), calls=%async_computation.13 | async-start | bytes 8388608
  349.3 4.0 slice-start.11
  349.3 4.0 copy-start.32
  370.2 21.6 %slice-start.6 = ((s8[6291456]{0:T(1024)(128)(4,1)}), s8[4194304]{0:T(1024)(128)(4,1)S(1)}, s32[]{:S(2)}) async-start(s8[6291456]{0:T(1024)(128)(4,1)} %bitcast.125), calls=%async_computation.9 | async-start | bytes 8388608
  370.2 21.6 %slice-start.7 = ((s8[6291456]{0:T(1024)(128)(4,1)}), s8[2097152]{0:T(1024)(128)(4,1)S(1)}, s32[]{:S(2)}) async-start(s8[6291456]{0:T(1024)(128)(4,1)} %bitcast.125), calls=%async_computation.10 | async-start | bytes 4194304
  386.7 5.2 copy-start.12
  391.9 9.4 %copy-start.42 = (f32[512]{0:T(512)S(1)}, f32[512]{0:T(512)}, u32[]{:S(2)}) copy-start(f32[512]{0:T(512)} %copy-done.41) | copy-start | bytes 6148
  401.3 7.6 %copy-start.16 = (f32[3,1024,512]{2,1,0:T(8,128)S(1)}, f32[3,1024,512]{2,1,0:T(8,128)}, u32[]{:S(2)}) copy-start(f32[3,1024,512]{2,1,0:T(8,128)} %get-tuple-element.40) | copy-start | bytes 18874372
  401.3 7.6 %copy-start.19 = (f32[1,1024,512]{2,1,0:T(8,128)S(1)}, f32[1,1024,512]{2,1,0:T(8,128)}, u32[]{:S(2)}) copy-start(f32[1,1024,512]{2,1,0:T(8,128)} %copy-done.18) | copy-start | bytes 6291460
  407.6 1.4 copy-start.31
  408.9 17.0 %copy-start.35 = (f32[512,512]{1,0:T(8,128)S(1)}, f32[512,512]{1,0:T(8,128)}, u32[]{:S(2)}) copy-start(f32[512,512]{1,0:T(8,128)} %convolution_bitcast_fusion.1) | copy-start | bytes 3145732
  408.9 17.0 %copy-start.36 = (f32[512,512]{1,0:T(8,128)S(1)}, f32[512,512]{1,0:T(8,128)}, u32[]{:S(2)}) copy-start(f32[512,512]{1,0:T(8,128)} %fusion.25) | copy-start | bytes 3145732
  408.9 17.0 %copy-start.37 = (f32[512,512]{1,0:T(8,128)S(1)}, f32[512,512]{1,0:T(8,128)}, u32[]{:S(2)}) copy-start(f32[512,512]{1,0:T(8,128)} %convolution_bitcast_fusion) | copy-start | bytes 3145732
  425.9 21.5 %slice-start.4 = ((s8[6291456]{0:T(1024)(128)(4,1)}), s8[2097152]{0:T(1024)(128)(4,1)S(1)}, s32[]{:S(2)}) async-start(s8[6291456]{0:T(1024)(128)(4,1)} %bitcast.122), calls=%async_computation.7 | async-start | bytes 4194304
  428.5 19.0 %slice-start.5 = ((s8[6291456]{0:T(1024)(128)(4,1)}), s8[4194304]{0:T(1024)(128)(4,1)S(1)}, s32[]{:S(2)}) async-start(s8[6291456]{0:T(1024)(128)(4,1)} %bitcast.122), calls=%async_computation.8 | async-start | bytes 8388608
  445.8 1.6 copy-start.20
  445.8 2.2 copy-start.22
  445.8 2.9 copy-start.24
  448.7 161.2 %copy-start.43 = (f32[192]{0:T(256)S(1)}, f32[192]{0:T(256)}, u32[]{:S(2)}) copy-start(f32[192]{0:T(256)} %param.17) | copy-start | bytes 2308
  448.7 161.2 %copy-start.44 = (f32[192]{0:T(256)S(1)}, f32[192]{0:T(256)}, u32[]{:S(2)}) copy-start(f32[192]{0:T(256)} %param.19) | copy-start | bytes 2308
  448.7 161.2 %copy-start.45 = (f32[192]{0:T(256)S(1)}, f32[192]{0:T(256)}, u32[]{:S(2)}) copy-start(f32[192]{0:T(256)} %param.21) | copy-start | bytes 2308
  448.7 161.9 %copy-start.38 = (f32[64,512]{1,0:T(8,128)S(1)}, f32[64,512]{1,0:T(8,128)}, u32[]{:S(2)}) copy-start(f32[64,512]{1,0:T(8,128)} %param.16) | copy-start | bytes 393220
  448.7 161.9 %copy-start.39 = (f32[64,512]{1,0:T(8,128)S(1)}, f32[64,512]{1,0:T(8,128)}, u32[]{:S(2)}) copy-start(f32[64,512]{1,0:T(8,128)} %param.18) | copy-start | bytes 393220
  448.7 161.9 %copy-start.40 = (f32[64,512]{1,0:T(8,128)S(1)}, f32[64,512]{1,0:T(8,128)}, u32[]{:S(2)}) copy-start(f32[64,512]{1,0:T(8,128)} %param.20) | copy-start | bytes 393220
Sparse Core Ops, SparseCore 0:
  10.9 65.4 all-gather.1
  428.6 139.8 reduce-scatter.1
where the time goes:
time: 630 us; the launch traced here: 621 us
  matrix products  219 us (35%)
  other arithmetic  131 us (21%)
  blocking collectives  118 us (19%)
  waiting for transfers between devices  83.2 us (13%)
  local copies, waits for them, and re-layouts  50 us (8%)
  between operations  19.2 us (3%)
    dot_general x16, matrix products, matmul(): return jnp.dot(left, right, precision=lax.Precision.HIGHEST)  219 us
    unnamed x2, blocking collectives  80.9 us
    reduce_scatter x1, waiting for transfers between devices, local(): lax.psum_scatter(grad_b, ('src', 'rcv'), scatter_dimension=0, tiled=True)  72.6 us
    mul x8, other arithmetic, pair_loss(): elu_slope(preact)[None] * mapped[1:]  43.7 us
    psum x1, blocking collectives, local(): total_sq = lax.psum(local_sq, ('src', 'rcv'))  37.1 us
    unnamed x133, local copies, waits for them, and re-layouts  35.4 us
    add x2, other arithmetic, pair_loss(): stream = stream + result  22.8 us
    reduce_sum x3, other arithmetic, pair_loss(): preact = mapped[0] + edge_table[7 + which]  16.6 us
  transfers between devices with their start and end apart: 2, of which 2 were waited for; matrix products, arithmetic and copies ran while one was open for 6% of the time, Pallas kernels for 0%

commit v1 on v0

v1 whole, which is shorter than its diff:
```python
import functools

import jax
import jax.numpy as jnp
from jax import lax
from jax.experimental import pallas as pl
from jax.experimental.pallas import tpu as pltpu
from jax.sharding import PartitionSpec as P

ADAM_STEP = 5
D = 512
CHUNK = 256
TILE = 64

clip_limit = 0.05
beta_one = 0.5
beta_two = 0.5
adam_eps = 1e-08
decay_rate = 0.01
block_rate = 0.02
edge_rate = 0.1

F32 = jnp.float32
BF16 = jnp.bfloat16
F8 = jnp.float8_e4m3fn
SMALL = pltpu.CompilerParams(vmem_limit_bytes=8 * 1024 * 1024)
NN = (((1,), (0,)), ((), ()))
NT = (((1,), (1,)), ((), ()))
AXES = ("k", "b", "x", "c")
FACTORS = 8 * D // 128


def dot(left, right, dims=NN):
    return lax.dot_general(left, right, dims, preferred_element_type=F32)


def split(x):
    high = x.astype(BF16)
    return high, (x - high.astype(F32)).astype(BF16)


def scale_of(bound):
    return 256.0 / jnp.maximum(bound, 1e-30)


def parts(x, scale):
    high = x.astype(BF16)
    left = (x - high.astype(F32)).astype(BF16)
    whole, left = high * scale.astype(BF16), left * (scale * 256.0).astype(BF16)
    return high, whole.astype(F8), left.astype(F8)


def largest(x):
    return jnp.max(jnp.abs(x), (0, 1), keepdims=True)


def tiles(stage, *arrays):
    cuts = [slice(at, at + TILE) for at in range(0, D, TILE)]
    done = [stage(*(one(cut) if callable(one) else one[cut] for one in arrays)) for cut in cuts]
    return tuple(jnp.concatenate(one, 0) for one in zip(*done))


def stack(x):
    return x.reshape(-1, 8, x.shape[1])


def top_of(x):
    return jnp.max(stack(jnp.abs(x)), 0)


def sum_of(x):
    return jnp.sum(stack(x), 0)


def weigh(weights, k, x):
    main, small, scales = weights
    high, whole, left, scale = x
    rest = dot(small[k], jnp.concatenate([left, whole], 0))
    return dot(main[k], high) + rest * (scales[k : k + 1, 0:1] / (256.0 * scale))


def outer(*terms):
    lefts, rights = ([one for term in terms for one in term[side]] for side in range(2))
    main = [jnp.concatenate([one[0] for one in side], 1) for side in (lefts, rights)]
    total = dot(*main, NT)
    for lefts, rights in terms:
        wide = jnp.concatenate([part for one in lefts for part in one[1:3]], 1)
        back = jnp.concatenate([part for one in rights for part in (one[2], one[1])], 1)
        total = total + dot(wide, back, NT) * (1.0 / (256.0 * lefts[0][3] * rights[0][3]))
    return total


def elu_parts(c):
    above = c > 0
    slope = jnp.exp(jnp.minimum(c, 0.0))
    curve = jnp.where(above, 0.0, jnp.where(c < 0, slope, 0.5))
    return jnp.where(above, c, slope - 1.0), slope, curve


def fold(x):
    total = x[:, :128]
    for at in range(128, x.shape[1], 128):
        total = total + x[:, at : at + 128]
    return total


def pair_kernel(layout, lanes, src_ref, rcv_ref, vel_ref, live_ref, near_ref, *refs):
    shared_edges = lanes != 4
    if shared_edges:
        e_ref, refs = refs[0], refs[1:]
    pieces, refs = refs[: len(layout)], refs[len(layout) :]
    aways, keeps, refs = refs[:lanes], refs[lanes : 2 * lanes], refs[2 * lanes :]
    small_ref, table_ref, dw_ref, full, left, et, limits, sums, wide, sems = refs[:10]
    wn, wt = refs[10:13], refs[13:16]
    rows = D // (2 * lanes)
    which, core = lax.axis_index("k"), lax.axis_index("c")
    lane = lax.axis_index(("b", "x"))

    shard = rows // 2 + (0 if shared_edges else 1)

    def matrix(k):
        lines = []
        for place in range(2 * lanes):
            first = (2 * lanes * k + place) * shard
            columns = [full[pl.ds(first + at, rows // 8, D // 128)] for at in range(D // 128)]
            lines.append(jnp.concatenate([one.reshape(rows, 128) for one in columns], 1))
        return jnp.concatenate(lines, 0)

    def edge_table():
        lines = []
        for at in range(4 * lanes):
            even, odd = (full[(2 * at + one) * shard + shard - 1] for one in range(2))
            lines += [even[0:1], even[1:2] + odd[0:1], odd[1:2]]
        wide_lines = [jnp.concatenate(lines[4 * at : 4 * at + 4], 1) for at in range(12)]
        return jnp.concatenate(wide_lines + [jnp.zeros((4, D), F32)], 0)

    def start(copies):
        copies = [pltpu.make_async_copy(a, b, sems.at[at]) for at, (a, b) in enumerate(copies)]
        for one in copies:
            one.start()
        return copies

    copies = []
    for ref, segments in zip(pieces, layout):
        for plane, other, swapped, at, first, size in segments:
            place = (lane ^ other) * 2 + (core ^ swapped)
            to = ((which ^ plane) * 2 * lanes + place) * shard + first
            to = full.at[pl.ds(to, size)]
            copies.append((ref.at[pl.ds(at, size)], to))
    for one in start(copies):
        one.wait()
    for k in range(3):
        plain = matrix(k + 1)
        for (main, small, scales), one in ((wn, plain), (wt, plain.T)):
            scale = scale_of(largest(one))
            main[k], small[k, :, :D], small[k, :, D:] = parts(one, scale)
            scales[k : k + 1] = jnp.broadcast_to(1.0 / scale, (1, 128))
            reach = jnp.max(jnp.sum(jnp.abs(one.T if main is wn[0] else plain), 0, keepdims=True))
            scales[4 + k : 5 + k] = jnp.full((1, 128), reach, F32)
    edge = e_ref[...] if shared_edges else edge_table()
    table_ref[...] = edge
    row = lax.broadcasted_iota(jnp.int32, (8, D), 0)
    first = jnp.where(row < 7, edge[:8], 0.0)
    fh, fl = split(first)
    wh, wl = split(matrix(0))
    mixed = dot(fh, wh) + dot(fh, wl) + dot(fl, wh)
    biased = mixed + jnp.where(row == 6, edge[7:8], 0.0)
    columns = jnp.concatenate([edge[8:12], edge[3:6], mixed[3:6], jnp.zeros((118, D), F32)], 0).T
    for at in range(10):
        et[at] = jnp.broadcast_to(columns[:, at : at + 1], (D, 128))
    rows_of = [edge[:8], biased, edge[8:16], mixed]
    for at, part in enumerate(rows_of):
        limits[8 * at : 8 * at + 8] = jnp.broadcast_to(
            jnp.max(jnp.abs(part), 1, keepdims=True), (8, 128)
        )
    tang = jnp.where(row < 3, pltpu.roll(first, 5, 0), 0.0)
    tang_mixed = jnp.where(row < 3, pltpu.roll(mixed, 5, 0), 0.0)
    for at, part in enumerate((first, biased, tang, tang_mixed)):
        high, low = split(part)
        cat = jnp.concatenate(
            [high.astype(F32), high.astype(F32), low.astype(F32), jnp.zeros((104, D), F32)], 0
        ).T
        left[at] = cat.astype(BF16)

    def column(at):
        return lambda cut: jnp.concatenate([et[at, cut]] * (CHUNK // 128), 1)

    chunks = range(rcv_ref.shape[2] // CHUNK)
    blocks = [(at, one) for at in range(src_ref.shape[0]) for one in chunks]

    def each(stage, *lists):
        return [stage(*one) for one in zip(*lists)]

    def both(stage, *lists):
        return tuple(zip(*each(stage, *lists)))

    def triple(x):
        high, low = (part.astype(F32) for part in split(x))
        return jnp.concatenate([high, low, high, jnp.zeros((104, CHUNK), F32)], 0).astype(BF16)

    def points(step, b):
        lanes_of = slice(b * CHUNK, (b + 1) * CHUNK)
        near = near_ref[pl.ds(step, 1), lanes_of] == 1
        source = src_ref[step]
        p = [jnp.concatenate([source[j : j + 1]] * (CHUNK // 128), 1) for j in range(3)]
        raw = [rcv_ref[j, pl.ds(step, 1), lanes_of] for j in range(3)]
        q = [jnp.where(near, a + 0.1 * b, b) for a, b in zip(p, raw)]
        ends = [jnp.ones((1, CHUNK), F32), jnp.zeros((1, CHUNK), F32)]
        return jnp.concatenate(p + q + ends, 0)

    x = [points(*one) for one in blocks]
    vel = [vel_ref[pl.ds(at, 1), b * CHUNK : (b + 1) * CHUNK] for at, b in blocks]
    live = [live_ref[pl.ds(at, 1), b * CHUNK : (b + 1) * CHUNK].astype(F32) for at, b in blocks]
    x_wide = each(triple, x)
    h0 = each(lambda one: dot(left[0], one), x_wide)
    a0 = each(lambda one: dot(left[1], one), x_wide)

    def reach(weights, k, x):
        return weights[2][4 + k : 5 + k, 0:1] * x

    def limit(at):
        return limits[at : at + 1, 0:1]

    def over_rows(first, count, x):
        sizes = jnp.max(jnp.abs(x[:count]), 1, keepdims=True)
        return jnp.sum(limits[first : first + count, 0:1] * sizes, 0, keepdims=True)

    def graded(stage, bounds, *lists):
        def run(scale, *arrays):
            def one(*cut):
                x, *rest = stage(*cut)
                high, whole, left = parts(x, scale)
                top = jnp.max(jnp.abs(high).reshape(-1, 16, CHUNK), 0).astype(F32)
                return (high, whole, left, top, *rest)

            high, whole, left, top, *rest = tiles(one, *arrays)
            return (high, whole, left, scale), largest(top), *rest

        scale = scale_of(functools.reduce(jnp.maximum, bounds))
        return both(run, again(scale), *lists)

    def again(one):
        return [one] * len(blocks)

    def enter(c, bias):
        return elu_parts(c + bias)

    def add_half(c, bias, h):
        v, s, k = elu_parts(c + bias)
        return h + v, s, k

    u0s, top, s0, k0 = graded(elu_parts, each(lambda x: over_rows(8, 7, x), x), a0)
    c1 = each(lambda one: weigh(wt, 0, one), u0s)
    bounds = each(lambda x, top: over_rows(0, 7, x) + reach(wt, 0, top) + limit(16), x, top)
    h1s, top, s1, k1, h1 = graded(
        lambda *one: (lambda h, s, k: (h, s, k, h))(*add_half(*one)), bounds, c1, again(column(0)), h0
    )
    a2 = each(lambda one: weigh(wt, 1, one), h1s)
    bounds = each(lambda top: reach(wt, 1, top) + limit(17), top)
    u2s, _, s2, k2 = graded(enter, bounds, a2, again(column(1)))
    c3 = each(lambda one: weigh(wt, 2, one), u2s)

    def last_half(c, bias, h, e):
        h, s, k = add_half(c, bias, h)
        return s * e, h, s, k, sum_of(h * e)

    e_top = limit(19)
    y3, top, h2, s3, k3, out = graded(last_half, again(e_top), c3, again(column(2)), h1, again(column(3)))
    out = each(lambda one: jnp.sum(one, 0, keepdims=True), out)

    l2 = each(lambda one: weigh(wn, 2, one), y3)
    bounds = each(lambda top: reach(wn, 2, top), top)
    y2, top, q2 = graded(lambda l, s, k: (s * l, l * k), bounds, l2, s2, k2)
    l1 = each(lambda one: weigh(wn, 1, one), y2)
    bounds = each(lambda top: reach(wn, 1, top) + e_top, top)

    def back_add(value, e, s, k):
        value = value + e
        return s * value, value, value * k

    y1, _, lh1, q1 = graded(back_add, bounds, l1, again(column(3)), s1, k1)
    l0 = each(lambda one: weigh(wn, 0, one), y1)

    def leave(value, s, k, h, *columns):
        y = s * value
        sums = [sum_of(h * columns[j] + y * columns[3 + j]) for j in range(3)]
        return y, value * k, *sums

    y0, q0, *slope = both(
        lambda *one: tiles(leave, *one, *(column(4 + j) for j in range(6))), l0, s0, k0, lh1
    )
    slope = each(
        lambda *one: jnp.concatenate([jnp.sum(part, 0, keepdims=True) for part in one], 0), *slope
    )

    def loss_slopes(x, vel, live, out, slope):
        p, q = x[0:3], x[3:6]
        ratio = jnp.sqrt(out * out + 1.0)
        part = out / ratio
        off = q - p
        dist = jnp.sqrt(jnp.sum(off * off, 0, keepdims=True) + 0.01)
        unit = off / dist
        grad = ratio * unit + dist * part * slope
        size = jnp.sqrt(jnp.sum(grad * grad, 0, keepdims=True) + 0.01)
        misfit = vel * size - 1.0
        d_grad = (2.0 * live * misfit * vel / size) * grad
        d_slope = d_grad * (dist * part)
        d_ratio = jnp.sum(d_grad * unit, 0, keepdims=True)
        d_part = jnp.sum(d_grad * slope, 0, keepdims=True) * dist
        inv = 1.0 / ratio
        d_out = d_ratio * part + d_part * (inv * inv * inv)
        return d_out, jnp.concatenate([d_slope, jnp.zeros((5, CHUNK), F32)], 0)

    d_out, om = both(loss_slopes, x, vel, live, out, slope)
    om_wide = each(triple, om)
    t0 = each(lambda one: dot(left[2], one), om_wide)
    m0 = each(lambda one: dot(left[3], one), om_wide)

    bounds = each(lambda om: over_rows(27, 3, om), om)
    du0, top, q0 = graded(lambda m, s, q: (s * m, m * q), bounds, m0, s0, q0)
    n1 = each(lambda one: weigh(wt, 0, one), du0)
    bounds = each(lambda om, top: over_rows(3, 3, om) + reach(wt, 0, top), om, top)

    def along_add(n, t, s, q):
        t = t + s * n
        q = n * q
        return t, t, q, top_of(q)

    t1s, top, t1, q1, q1_top = graded(along_add, bounds, n1, t0, s1, q1)
    m2 = each(lambda one: weigh(wt, 1, one), t1s)

    def along(m, s, q):
        q = m * q
        return s * m, q, top_of(q)

    bounds = each(lambda top: reach(wt, 1, top), top)
    du2, top, q2, q2_top = graded(along, bounds, m2, s2, q2)
    n3 = each(lambda one: weigh(wt, 2, one), du2)

    def turn(n, s, k, t, h, e, d):
        cb = e * (d * s + n * k)
        return cb, fold(cb), fold(d * h + t + s * n)

    def down(u, s, q):
        ab = u * s + q
        return ab, fold(ab)

    def down_add(u, e, s, q, lh, d, x, om):
        hb = u + d * e
        cb = hb * s + q
        return cb, fold(cb), fold(hb), *weighted(hb, lh, x, om)

    def end(u, s, q, y, x, om):
        ab = u * s + q
        return fold(ab), *weighted(ab, y, x, om)

    def weighted(value, other, x, om):
        return [fold(value * x[3 + j : 4 + j] + other * om[j : j + 1]) for j in range(3)]

    def same(one):
        return lambda cut: one

    d_top = each(largest, d_out)
    d_all, x_all, om_all = (each(same, one) for one in (d_out, x, om))
    bounds = each(lambda d, top: e_top * (d + reach(wt, 2, top)), d_top, top)
    cb3, top, *sum3 = graded(turn, bounds, n3, s3, k3, t1, h2, again(column(3)), d_all)
    ub2 = each(lambda one: weigh(wn, 2, one), cb3)
    dw_ref[2] = outer((u2s, cb3), (du2, y3))
    bounds = each(lambda top, q: reach(wn, 2, top) + largest(q), top, q2_top)
    ab2, top, *sum2 = graded(down, bounds, ub2, s2, q2)
    hb1 = each(lambda one: weigh(wn, 1, one), ab2)
    dw_ref[1] = outer((h1s, ab2), (t1s, y2))
    bounds = each(lambda d, top, q: e_top * d + reach(wn, 1, top) + largest(q), d_top, top, q1_top)
    cb1, _, *sum1 = graded(down_add, bounds, hb1, again(column(3)), s1, q1, lh1, d_all, x_all, om_all)
    ub0 = each(lambda one: weigh(wn, 0, one), cb1)
    dw_ref[0] = outer((u0s, cb1), (du0, y1))
    sum0 = both(
        lambda u, s, q, y, a, b: tiles(end, u, s, q, y, same(a), same(b)), ub0, s0, q0, y0, x, om
    )
    for at, terms in enumerate((sum1[0], sum2[0], sum3[0], sum3[1])):
        sums[at] = sum(terms)
    for at, (ones, *points_of) in enumerate((sum0, sum1[1:])):
        wide[at, 6] = sum(ones)
        for j in range(3):
            wide[at, j] = sum(src_ref[one, j : j + 1] * part for (one, _), part in zip(blocks, ones))
            wide[at, 3 + j] = sum(points_of[j])

    copies = []
    for half, refs in ((1 - core, aways), (core, keeps)):
        for other in reversed(range(lanes)):
            first = pl.multiple_of((2 * (lane ^ other) + half) * rows, 8)
            for k in range(3):
                there = refs[other].at[pl.ds(k * rows, rows)]
                copies.append((dw_ref.at[k, pl.ds(first, rows)], there))
    copies = start(copies)

    row = lax.broadcasted_iota(jnp.int32, (8, D), 0)

    def gather(at):
        lines = [jnp.sum(wide[at, one].T, 0, keepdims=True) for one in range(7)]
        return jnp.concatenate(lines + [jnp.zeros((1, D), F32)], 0)

    g, h = gather(0), gather(1)
    gh_, gl_ = split(g)
    wh, wl = split(matrix(0))
    first = h + dot(gh_, wh, NT) + dot(gh_, wl, NT) + dot(gl_, wh, NT)
    first = jnp.where(row < 7, first, g[6:7])
    tails = [jnp.sum(sums[at].T, 0, keepdims=True) for at in range(4)]
    small_ref[0:8] = first
    small_ref[8:16] = jnp.concatenate(tails + [jnp.zeros((4, D), F32)], 0)
    small_ref[16:24] = jnp.where(row < 7, g, 0.0)
    for one in copies:
        one.wait()


def pair_grads(pairs, edges, pieces, layout, lanes):
    rows = D // (2 * lanes)
    sent = [jax.ShapeDtypeStruct((3 * rows, D), F32)] * (2 * lanes)
    count = pairs[1].shape[1] * pairs[1].shape[2]
    segments = sum(len(one) for one in layout)
    vmem, held = pl.BlockSpec(memory_space=pltpu.VMEM), pl.BlockSpec(memory_space=pl.ANY)
    outs = pl.pallas_call(
        functools.partial(pair_kernel, layout, lanes),
        in_specs=[vmem] * (5 + len(edges)) + [held] * len(pieces),
        out_specs=[held] * len(sent) + [vmem] * 2,
        out_shape=sent
        + [jax.ShapeDtypeStruct((24, D), F32), jax.ShapeDtypeStruct((16, D), F32)],
        scratch_shapes=[
            pltpu.VMEM((3, D, D), F32),
            pltpu.VMEM((8 * lanes * (rows // 2 + (lanes == 4)), 8, 128), F32),
            pltpu.VMEM((4, D, 128), BF16),
            pltpu.VMEM((10, D, 128), F32),
            pltpu.VMEM((32, 128), F32),
            pltpu.VMEM((4, D, 128), F32),
            pltpu.VMEM((2, 7, D, 128), F32),
            pltpu.SemaphoreType.DMA((max(segments, 6 * lanes),)),
        ]
        + [
            pltpu.VMEM((3, D, D), BF16),
            pltpu.VMEM((3, D, 2 * D), F8),
            pltpu.VMEM((8, 128), F32),
        ]
        * 2,
        compiler_params=pltpu.CompilerParams(vmem_limit_bytes=60 * 1024 * 1024),
        cost_estimate=pl.CostEstimate(
            flops=54 * 2 * count * D * D, bytes_accessed=8 * 1024 * 1024, transcendentals=4 * count * D
        ),
    )(*pairs, *edges, *pieces)
    return outs[:lanes], outs[lanes : 2 * lanes], *outs[2 * lanes :]


def adamw(weights, grads, first, second, rate):
    first_new = beta_one * first + (1.0 - beta_one) * grads
    second_new = beta_two * second + (1.0 - beta_two) * grads * grads
    first_hat = first_new / (1.0 - beta_one**ADAM_STEP)
    second_hat = second_new / (1.0 - beta_two**ADAM_STEP)
    weights_new = weights - rate * (
        first_hat / (jnp.sqrt(second_hat) + adam_eps) + decay_rate * weights
    )
    return (weights_new, first_new, second_new)


def exchange(x, plane, other, swapped, lanes):
    total = 8 * lanes
    mask = (plane * lanes + other) * 2 + swapped
    return lax.ppermute(x, AXES, [(i, i ^ mask) for i in range(total)])


def in_turn(first, *others):
    done = (first,)
    for one in others:
        one, *done = lax.optimization_barrier((one, *done))
        done = (*done, one)
    return done


def as_tiles(own):
    rows = own.shape[0]
    tiled = own.reshape(rows // 8, 8, D // 128, 128).transpose(0, 2, 1, 3)
    return tiled.reshape(rows // 2, 8, 128)


def spread(own, edges, sources, lanes):
    size = own.shape[0] // 2 + (lanes == 4)
    own = as_tiles(own)

    def at(plane, other, first=0):
        return [(plane, other, 0, first, 0, size)]

    def to_core(array):
        return exchange(array, 0, 0, 1, lanes)

    def to_place(array, other):
        return exchange(array, 0, other, 0, lanes)

    if lanes != 4:
        far = [exchange(own, plane, 0, 0, lanes) for plane in (1, 2, 3)]
        stack = jnp.concatenate([own] + far, 0)
        got = [
            (to_place(stack, other) if other else stack, sum((at(p, other, p * size) for p in range(4)), []))
            for other in range(lanes)
        ]
        swaps = [to_core(array) for array, _ in got]
    else:
        odd = lax.axis_index("c") == 1
        line = jnp.where(odd, jnp.pad(edges, (64, 0)), jnp.pad(edges, (0, 64)))
        line = jnp.pad(line.reshape(1, 2, 128), ((0, 0), (0, 6), (0, 0)))
        own = jnp.concatenate([own, line], 0)
        far = [exchange(own, plane, 0, 0, lanes) for plane in (1, 2, 3)]
        near = [to_place(own, other) for other in (1, 2)]
        diagonal = to_place(own, 3)
        far[0], sources, far[1], far[2], near[1], near[0], diagonal = in_turn(
            far[0], sources, far[1], far[2], near[1], near[0], diagonal
        )
        early = [own, *near, diagonal]
        stack = jnp.concatenate(far, 0)
        more = [to_place(stack, other) for other in (1, 2)]
        swaps = [to_core(array) for array in early[:3]]
        ahead = more[1]
        more[1], more[0], *swaps = in_turn(more[1], more[0], *swaps)
        half = 3 * size // 2
        ends = [to_place(ahead[:half], 1), to_place(more[0][half:], 2)]
        swaps += [to_core(array) for array in (diagonal, stack, *more)]
        tied = in_turn(*ends, *swaps)
        ends, swaps = tied[:2], list(tied[2:])

        def three(other):
            return sum((at(p, other, (p - 1) * size) for p in (1, 2, 3)), [])

        def cut(segments, low, high):
            found = []
            for plane, other, core, here, first, count in segments:
                start, stop = max(here, low), min(here + count, high)
                if start < stop:
                    found.append((plane, other, core, start - low, first + start - here, stop - start))
            return found

        got = [(array, at(0, other)) for other, array in enumerate(early)]
        got += [(stack, three(0)), (more[0], three(1)), (more[1], three(2))]
        got += [(ends[0], cut(three(3), 0, half)), (ends[1], cut(three(3), half, 3 * size))]
        swaps += [to_core(array) for array in ends]
    got += [
        (array, [(a, b, 1, *rest) for a, b, _, *rest in segments])
        for array, (_, segments) in zip(swaps, list(got))
    ]
    return [array for array, _ in got], [tuple(segments) for _, segments in got], sources


def local(
    lanes,
    src_coords,
    rcv_coords,
    velocity,
    pair_mask,
    near_flag,
    block_params,
    edge_params,
    block_moment,
    edge_moment,
    block_second,
    edge_second,
):
    plane = 2 * lanes
    total = 4 * plane
    rows = block_params.shape[0]
    which, core = lax.axis_index("k"), lax.axis_index("c")
    me = lax.axis_index(AXES)

    def to_all(x):
        return lax.all_to_all(x, AXES, 0, 0, tiled=True)

    share = edge_params.shape[0]
    sources = jnp.broadcast_to(src_coords.T.reshape(-1, 3, 1), (src_coords.shape[1], 3, 128))
    edges = []
    if lanes != 4:
        edges = to_all(jnp.broadcast_to(edge_params[None, None], (total, 1, share)))
        edges = [jnp.pad(edges.reshape(12, D), ((0, 4), (0, 0)))]
    pieces, layout, sources = spread(block_params, edge_params, sources, lanes)
    pairs = (sources, rcv_coords, velocity, pair_mask, near_flag)
    away, keep, small, edges = pair_grads(pairs, edges, pieces, layout, lanes)

    arrived = []
    for other in reversed(range(lanes)):
        part = keep[other] + exchange(away[other], 0, 0, 1, lanes)
        arrived.append(exchange(part, 0, other, 0, lanes) if other else part)
    arrived = [*in_turn(*arrived[:-1]), arrived[-1]]
    shares = [small[:12].reshape(total, 1, share), small[16:24].reshape(FACTORS, 1, -1)]
    shares[1] = jnp.pad(shares[1], ((0, total - FACTORS), (0, 0), (0, 0)))
    shares = to_all(jnp.concatenate(shares, 2))

    arrived[0], shares = lax.optimization_barrier((arrived[0], shares))

    def rows_of(matrix):
        at = jnp.maximum(matrix - 1, 0) * rows
        return sum(lax.dynamic_slice_in_dim(one, at, rows, 0) for one in arrived)

    owned = []
    for other in (3, 2, 1):
        perm = [(i, i ^ (other * plane)) for i in range(total)]
        owned.append(lax.ppermute(rows_of(which ^ other), AXES, perm))
    owned = [*in_turn(*owned), rows_of(which)]

    kind = which.astype(jnp.int32).reshape(1)
    owned, own_edges, shared = collect(kind, owned, shares, pair_mask, share)
    shared = to_all(shared)
    own_first = lax.dynamic_slice_in_dim(edges[:8], me % plane * rows, rows, 1).T
    return update(
        kind,
        (shared, edges[:8], own_first),
        (owned, block_params, block_moment, block_second),
        (own_edges, edge_params, edge_moment, edge_second),
    )


def collect_kernel(kind_ref, shares_ref, mask_ref, *refs):
    owned_ref, edges_ref, shared_ref = refs[-3:]
    share = edges_ref.shape[1]
    kind = kind_ref[0]

    owned_ref[...] = jnp.where(kind == 0, 0.0, sum(one[...] for one in refs[:-3]))
    shares = jnp.sum(shares_ref[...], 0)
    own = shares[:, :share]
    edges_ref[...] = own

    def whole(x):
        return jnp.sum(jnp.sum(x, 0, keepdims=True), 1, keepdims=True)

    squares = whole(owned_ref[...] * owned_ref[...]) + whole(own * own)
    live = whole(mask_ref[...].astype(F32))
    lane = lax.broadcasted_iota(jnp.int32, (1, 128), 1)
    sums = jnp.where(lane == 0, squares, jnp.where(lane == 1, live, 0.0))
    line = jnp.concatenate([sums, shares[:, share:]], 1)
    shared_ref[...] = jnp.broadcast_to(line[None], shared_ref.shape)


def collect(kind, owned, shares, mask, share):
    rows, total = owned[0].shape[0], shares.shape[0]
    smem, vmem = pl.BlockSpec(memory_space=pltpu.SMEM), pl.BlockSpec(memory_space=pltpu.VMEM)
    shapes = [(rows, D), (1, share), (total, 1, 256)]
    return pl.pallas_call(
        collect_kernel,
        in_specs=[smem] + [vmem] * (2 + len(owned)),
        out_specs=[vmem] * 3,
        out_shape=[jax.ShapeDtypeStruct(one, F32) for one in shapes],
        compiler_params=SMALL,
    )(kind, shares, mask, *owned)


def update_kernel(kind_ref, shared_ref, edge_ref, own_ref, *refs):
    ins, outs = refs[:8], refs[8:]
    shared = jnp.sum(shared_ref[:, :, :128], 0)
    lane = lax.broadcasted_iota(jnp.int32, shared.shape, 1)
    per = D // 128
    lines = [
        jnp.concatenate([shared_ref[at * per + one, :, 128:] for one in range(per)], 1)
        for at in range(8)
    ]
    factor, rows, own = jnp.concatenate(lines, 0), edge_ref[...], own_ref[...]
    first = jnp.zeros(ins[0].shape, F32)
    mixed = jnp.zeros_like(factor)
    for at in range(7):
        first = first + own[:, at : at + 1] * factor[at : at + 1]
        gram = jnp.sum(rows * rows[at : at + 1], 1, keepdims=True)
        mixed = mixed + gram * factor[at : at + 1]
    valid = lax.broadcasted_iota(jnp.int32, factor.shape, 0) < 7
    first_sq = jnp.sum(jnp.where(valid, mixed * factor, 0.0), 0, keepdims=True)
    first_sq = jnp.sum(first_sq, 1, keepdims=True)
    total_sq = jnp.sum(jnp.where(lane == 0, shared, 0.0), 1, keepdims=True) + first_sq
    count = jnp.sum(jnp.where(lane == 1, shared, 0.0), 1, keepdims=True)
    count = jnp.maximum(count, 1.0)
    grad_norm = jnp.sqrt(total_sq) / count
    outs[0][0] = grad_norm[0, 0]
    scale = jnp.minimum(1.0, clip_limit / (grad_norm + 1e-06)) / count
    for at, rate in ((0, block_rate), (4, edge_rate)):
        raw, weights, one, two = (ref[...] for ref in ins[at : at + 4])
        if at == 0:
            raw = jnp.where(kind_ref[0] == 0, first, raw)
        weights, one, two = adamw(weights, raw * scale, one, two, rate)
        outs[1 + at][...] = weights
        outs[2 + at][...] = one
        outs[3 + at][...] = two
        low = weights.astype(BF16)
        outs[4 + at][...] = low.reshape(outs[4 + at].shape)


def update(kind, shared, blocks, edges):
    edges = (edges[0],) + tuple(one[None] for one in edges[1:])
    smem, vmem = pl.BlockSpec(memory_space=pltpu.SMEM), pl.BlockSpec(memory_space=pltpu.VMEM)
    shapes = [(1,)] + [blocks[0].shape] * 4 + [edges[0].shape] * 3 + [edges[0].shape[1:]]
    types = [F32] + [F32, F32, F32, BF16] * 2
    outs = pl.pallas_call(
        update_kernel,
        in_specs=[smem] + [vmem] * 11,
        out_specs=[smem] + [vmem] * 8,
        out_shape=[jax.ShapeDtypeStruct(a, b) for a, b in zip(shapes, types)],
        compiler_params=SMALL,
    )(kind, *shared, *blocks, *edges)
    norm, new_b, moment_b, second_b, low_b, new_e, moment_e, second_e, low_e = outs
    new_e, moment_e, second_e = (one[0] for one in (new_e, moment_e, second_e))
    return norm.reshape(()), new_b, new_e, moment_b, moment_e, second_b, second_e, low_b, low_e


def solution(mesh):
    count_src, count_rcv = mesh.shape["src"], mesh.shape["rcv"]
    shape = (4, count_src // 4, count_rcv // 2, 2)
    split_mesh = jax.sharding.Mesh(mesh.devices.reshape(shape), AXES)
    src, rcv = ("k", "b"), ("x", "c")
    wide, flat = P(AXES, None), P(AXES)
    placed = (
        P(None, src),
        P(None, src, rcv),
        P(src, rcv),
        P(src, rcv),
        P(src, rcv),
        wide,
        flat,
        wide,
        flat,
        wide,
        flat,
    )
    return jax.shard_map(
        functools.partial(local, shape[1] * shape[2]),
        mesh=split_mesh,
        in_specs=placed,
        out_specs=(P(), wide, flat, wide, flat, wide, flat, wide, flat),
        check_vma=False,
    )
```

time: 630 us -> 129 us (0.20); the launches traced: 621 us -> 129 us
  matrix products: 219 us -> 0 us
  other arithmetic: 131 us -> 4 us
  blocking collectives: 118 us -> 0 us
  local copies, waits for them, and re-layouts: 50 us -> 3.8 us
  starting transfers between devices: 0.08 us -> 38.4 us
  waiting for transfers between devices: 83.2 us -> 45.4 us
  Pallas kernels: 0 us -> 35.7 us
  between operations: 19.2 us -> 1.29 us
    dot_general x16 -> x0, matrix products: 219 us -> none  [matmul(): return jnp.dot(left, right, precision=lax.Precision.HIGHEST)]
    unnamed x2 -> x0, blocking collectives: 80.9 us -> none
    reduce_scatter x1 -> x0, waiting for transfers between devices: 72.6 us -> none  [local(): lax.psum_scatter(grad_b, ('src', 'rcv'), scatter_dimension=0, tiled=True)]
    mul x9 -> x0, other arithmetic: 43.7 us -> none  [the longest x8 43.7 us: pair_loss(): elu_slope(preact)[None] * mapped[1:]]
    ppermute x0 -> x29, waiting for transfers between devices: none -> 38.1 us  [the longest x26 28.9 us: exchange(): return lax.ppermute(x, AXES, [(i, i ^ mask) for i in range(total)])]
    psum x1 -> x0, blocking collectives: 37.1 us -> none  [local(): total_sq = lax.psum(local_sq, ('src', 'rcv'))]
    pallas_call x0 -> x3, Pallas kernels: none -> 35.7 us  [the longest x1 33.8 us: pair_grads(): pl.pallas_call(functools.partial(pair_kernel, layout, lanes), in_specs=[v...]
    unnamed x133 -> x64, local copies, waits for them, and re-layouts: 35.4 us -> 2.75 us
  transfers between devices with their start and end apart: 2 -> 31, of which waited for: 2 -> 13; matrix products, arithmetic and copies ran while one was open for 6% -> 3% of each run, Pallas kernels for 0% -> 0%
where the time goes in v1:
time: 129 us
  waiting for transfers between devices  45.4 us (35%)
  starting transfers between devices  38.4 us (30%)
  Pallas kernels  35.7 us (28%)
  other arithmetic  4 us (3%)
  local copies, waits for them, and re-layouts  3.8 us (3%)
  between operations  1.29 us (1%)
    pallas_call x1, Pallas kernels, pair_grads(): pl.pallas_call(functools.partial(pair_kernel, layout, lanes), in_specs=[v...  33.8 us
    ppermute x26, waiting for transfers between devices, exchange(): return lax.ppermute(x, AXES, [(i, i ^ mask) for i in range(total)])  28.9 us
    ppermute x26, starting transfers between devices, exchange(): return lax.ppermute(x, AXES, [(i, i ^ mask) for i in range(total)])  22.6 us
    all_to_all x2, starting transfers between devices, to_all(): return lax.all_to_all(x, AXES, 0, 0, tiled=True)  10 us
    ppermute x3, waiting for transfers between devices, local(): owned.append(lax.ppermute(rows_of(which ^ other), AXES, perm))  9.26 us
    all_to_all x2, waiting for transfers between devices, to_all(): return lax.all_to_all(x, AXES, 0, 0, tiled=True)  7.33 us
    ppermute x3, starting transfers between devices, local(): owned.append(lax.ppermute(rows_of(which ^ other), AXES, perm))  5.79 us
    unnamed x64, local copies, waits for them, and re-layouts  2.75 us
  transfers between devices with their start and end apart: 31, of which 13 were waited for; matrix products, arithmetic and copies ran while one was open for 3% of the time, Pallas kernels for 0%

profile of v1, /device:TPU:0, one launch (start us, length us, event | category | flops | bytes accessed | tf_op | source)
XLA Modules:
  0.0 128.7 jit_solution(13717088656755012168)
XLA Ops:
  0.7 0.7 copy-done.4
  1.3 0.1 select_bitcast_fusion
  1.4 0.9 select_maximum_fusion.refs_0_
  2.3 0.0 copy-start.16
  2.3 3.1 %collective-permute-start.5 = (f32[33,8,128]{2,1,0:T(8,128)S(1)}, f32[33,8,128]{2,1,0:T(8,128)S(1)}, u32[]{:S(2)}, u32[]{:S(2)}) collective-permute-start(f32[33,8,128]{2,1,0:T(8,128)S(1)} %select_maximum_fusion.refs_0_), channel_id=1, source_target_pairs={{0,8},{1,9},{2,10},{3,11},{4,12},{5,13},{6,14},{7,15},{8,0},{9,1},... | collective-permute-start | bytes 405512 | tf_op jit(solution)/shard_map/ppermute | solution.py:466
  5.4 2.6 %collective-permute-start.4 = (f32[33,8,128]{2,1,0:T(8,128)S(1)}, f32[33,8,128]{2,1,0:T(8,128)S(1)}, u32[]{:S(2)}, u32[]{:S(2)}) collective-permute-start(f32[33,8,128]{2,1,0:T(8,128)S(1)} %select_maximum_fusion.refs_0_), channel_id=1, source_target_pairs={{0,16},{1,17},{2,18},{3,19},{4,20},{5,21},{6,22},{7,23},{8,24},{9,... | collective-permute-start | bytes 405512 | tf_op jit(solution)/shard_map/ppermute | solution.py:466
  8.0 0.0 collective-permute-start.3
  8.0 1.7 %collective-permute-start.2 = (f32[33,8,128]{2,1,0:T(8,128)S(1)}, f32[33,8,128]{2,1,0:T(8,128)S(1)}, u32[]{:S(2)}, u32[]{:S(2)}) collective-permute-start(f32[33,8,128]{2,1,0:T(8,128)S(1)} %select_maximum_fusion.refs_0_), channel_id=1, source_target_pairs={{0,4},{1,5},{2,6},{3,7},{4,0},{5,1},{6,2},{7,3},{8,12},{9,13},{10,... | collective-permute-start | bytes 405512 | tf_op jit(solution)/shard_map/ppermute | solution.py:466
  9.8 1.5 %collective-permute-start.1 = (f32[33,8,128]{2,1,0:T(8,128)S(1)}, f32[33,8,128]{2,1,0:T(8,128)S(1)}, u32[]{:S(2)}, u32[]{:S(2)}) collective-permute-start(f32[33,8,128]{2,1,0:T(8,128)S(1)} %select_maximum_fusion.refs_0_), channel_id=1, source_target_pairs={{0,2},{1,3},{2,0},{3,1},{4,6},{5,7},{6,4},{7,5},{8,10},{9,11},{10,... | collective-permute-start | bytes 405512 | tf_op jit(solution)/shard_map/ppermute | solution.py:466
  11.3 0.0 collective-permute-done.5
  11.3 2.1 %collective-permute-start = (f32[33,8,128]{2,1,0:T(8,128)S(1)}, f32[33,8,128]{2,1,0:T(8,128)S(1)}, u32[]{:S(2)}, u32[]{:S(2)}) collective-permute-start(f32[33,8,128]{2,1,0:T(8,128)S(1)} %select_maximum_fusion.refs_0_), channel_id=1, source_target_pairs={{0,6},{1,7},{2,4},{3,5},{4,2},{5,3},{6,0},{7,1},{8,14},{9,15},{10,... | collective-permute-start | bytes 405512 | tf_op jit(solution)/shard_map/ppermute | solution.py:466
  13.3 0.7 broadcast_in_dim.14.src_ref
  14.0 4.6 %collective-permute-done.4 = f32[33,8,128]{2,1,0:T(8,128)S(1)} collective-permute-done((f32[33,8,128]{2,1,0:T(8,128)S(1)}, f32[33,8,128]{2,1,0:T(8,128)S(1)}, u32[]{:S(2)}, u32[]{:S(2)}) %collective-permute-start.4) | collective-permute-done | bytes 135200 | tf_op jit(solution)/shard_map/ppermute | solution.py:466
  18.6 0.0 collective-permute-done.3
  18.8 1.6 %collective-permute-start.10 = (f32[99,8,128]{2,1,0:T(8,128)S(1)}, f32[99,8,128]{2,1,0:T(8,128)S(1)}, u32[]{:S(2)}, u32[]{:S(2)}) collective-permute-start(f32[99,8,128]{2,1,0:T(8,128)S(1)} %constant_dynamic-update-slice_fusion.refs_4_), channel_id=1, source_target_pairs={{0,4},{1,5},{2,6},{3,7},{4,0},{5,1},{6,2},{7,3},{8,12},{9,13},{10,... | collective-permute-start | bytes 1216520 | tf_op jit(solution)/shard_map/ppermute | solution.py:466
  20.3 1.5 %collective-permute-start.9 = (f32[99,8,128]{2,1,0:T(8,128)S(1)}, f32[99,8,128]{2,1,0:T(8,128)S(1)}, u32[]{:S(2)}, u32[]{:S(2)}) collective-permute-start(f32[99,8,128]{2,1,0:T(8,128)S(1)} %constant_dynamic-update-slice_fusion.refs_4_), channel_id=1, source_target_pairs={{0,2},{1,3},{2,0},{3,1},{4,6},{5,7},{6,4},{7,5},{8,10},{9,11},{10,... | collective-permute-start | bytes 1216520 | tf_op jit(solution)/shard_map/ppermute | solution.py:466
  21.8 0.5 collective-permute-start.7
  22.3 0.1 collective-permute-start.6
  22.4 5.2 %collective-permute-done.10.refs_6_ = f32[99,8,128]{2,1,0:T(8,128)S(1)} collective-permute-done((f32[99,8,128]{2,1,0:T(8,128)S(1)}, f32[99,8,128]{2,1,0:T(8,128)S(1)}, u32[]{:S(2)}, u32[]{:S(2)}) %collective-permute-start.10) | collective-permute-done | bytes 405536 | tf_op jit(solution)/shard_map/ppermute | solution.py:466
  27.7 1.0 collective-permute-done.9.refs_5_
  28.7 0.1 collective-permute-start.12
  28.8 0.5 collective-permute-start.11
  29.3 1.6 %collective-permute-start.16 = (f32[49,8,128]{2,1,0:T(8,128)S(1)}, f32[49,8,128]{2,1,0:T(8,128)S(1)}, u32[]{:S(2)}, u32[]{:S(2)}) collective-permute-start(f32[49,8,128]{2,1,0:T(8,128)S(1)} %slice.21), channel_id=1, source_target_pairs={{0,2},{1,3},{2,0},{3,1},{4,6},{5,7},{6,4},{7,5},{8,10},{9,11},{10,... | collective-permute-start | bytes 602120 | tf_op jit(solution)/shard_map/ppermute | solution.py:466
  31.0 0.6 collective-permute-start.15
  31.5 4.8 %collective-permute-done.16.refs_7_ = f32[49,8,128]{2,1,0:T(8,128)S(1)} collective-permute-done((f32[49,8,128]{2,1,0:T(8,128)S(1)}, f32[49,8,128]{2,1,0:T(8,128)S(1)}, u32[]{:S(2)}, u32[]{:S(2)}) %collective-permute-start.16) | collective-permute-done | bytes 200736 | tf_op jit(solution)/shard_map/ppermute | solution.py:466
  36.4 1.4 %collective-permute-done.15.refs_8_ = f32[50,8,128]{2,1,0:T(8,128)S(1)} collective-permute-done((f32[50,8,128]{2,1,0:T(8,128)S(1)}, f32[50,8,128]{2,1,0:T(8,128)S(1)}, u32[]{:S(2)}, u32[]{:S(2)}) %collective-permute-start.15) | collective-permute-done | bytes 204832 | tf_op jit(solution)/shard_map/ppermute | solution.py:466
  37.9 0.1 collective-permute-start.18
  38.0 0.5 collective-permute-start.17
  38.5 1.2 collective-permute-done.17.refs_16_
  39.8 0.6 copy-done.23
  40.4 0.7 copy-done.21
  41.0 33.8 %shard_map.178 = (f32[192,512]{1,0:T(8,128)}, f32[192,512]{1,0:T(8,128)}, f32[192,512]{1,0:T(8,128)}, f32[192,512]{1,0:T(8,128)}, f32[192,512]{1,0:T(8,128)}, /*...) custom-call(f32[2,3,128]{2,1,0:T(4,128)} %broadcast_in_dim.14.src_ref,, ...), custom_call_target="tpu_custom_call" | custom-call | flops 28991029248 | bytes 8388608 | tf_op jit(solution)/shard_map/pallas_call | solution.py:422
  74.8 0.3 collective-permute-start.23
  75.1 0.3 collective-permute-start.21
  75.4 0.2 collective-permute-start.19
  75.6 0.3 collective-permute-start.25
  75.9 0.9 collective-permute-done.23
  76.8 1.1 add.100
  77.9 1.6 %collective-permute-start.24 = (f32[192,512]{1,0:T(8,128)S(1)}, f32[192,512]{1,0:T(8,128)S(1)}, u32[]{:S(2)}, u32[]{:S(2)}) collective-permute-start(f32[192,512]{1,0:T(8,128)S(1)} %add.100), channel_id=1, source_target_pairs={{0,6},{1,7},{2,4},{3,5},{4,2},{5,3},{6,0},{7,1},{8,14},{9,15},{10,... | collective-permute-start | bytes 1179656 | tf_op jit(solution)/shard_map/ppermute | solution.py:466
  79.6 0.1 add.99
  79.6 1.4 %collective-permute-start.22 = (f32[192,512]{1,0:T(8,128)S(1)}, f32[192,512]{1,0:T(8,128)S(1)}, u32[]{:S(2)}, u32[]{:S(2)}) collective-permute-start(f32[192,512]{1,0:T(8,128)S(1)} %add.99), channel_id=1, source_target_pairs={{0,4},{1,5},{2,6},{3,7},{4,0},{5,1},{6,2},{7,3},{8,12},{9,13},{10,... | collective-permute-start | bytes 1179656 | tf_op jit(solution)/shard_map/ppermute | solution.py:466
  81.0 0.8 add.98
  81.8 0.6 collective-permute-start.20
  82.4 0.1 reshape.45
  82.6 0.8 pad_maximum_fusion
  83.3 6.1 %all-to-all-start = ((f32[32,1,320]{2,1,0:T(1,128)}), f32[32,1,320]{2,1,0:T(1,128)S(1)}, u32[]{:S(2)}, u32[]{:S(2)}) async-start(f32[32,1,320]{2,1,0:T(1,128)} %pad_maximum_fusion), calls=%async_computation | async-start | bytes 98304 | tf_op jit(solution)/shard_map/all_to_all | solution.py:570
  89.4 0.1 add.104
  89.5 1.4 %collective-permute-done.24 = f32[192,512]{1,0:T(8,128)S(1)} collective-permute-done((f32[192,512]{1,0:T(8,128)S(1)}, f32[192,512]{1,0:T(8,128)S(1)}, u32[]{:S(2)}, u32[]{:S(2)}) %collective-permute-start.24) | collective-permute-done | bytes 393248 | tf_op jit(solution)/shard_map/ppermute | solution.py:466
  90.9 8.1 %collective-permute-done.22 = f32[192,512]{1,0:T(8,128)S(1)} collective-permute-done((f32[192,512]{1,0:T(8,128)S(1)}, f32[192,512]{1,0:T(8,128)S(1)}, u32[]{:S(2)}, u32[]{:S(2)}) %collective-permute-start.22) | collective-permute-done | bytes 393248 | tf_op jit(solution)/shard_map/ppermute | solution.py:466
  99.0 0.1 all-to-all-done.shares_ref
  99.1 0.2 dynamic-slice_add_fusion
  99.3 0.0 copy-start.15
  99.3 4.6 %collective-permute-start.27 = (f32[64,512]{1,0:T(8,128)S(1)}, f32[64,512]{1,0:T(8,128)S(1)}, u32[]{:S(2)}, u32[]{:S(2)}) collective-permute-start(f32[64,512]{1,0:T(8,128)S(1)} %get-tuple-element.249), channel_id=1, source_target_pairs={{0,16},{1,17},{2,18},{3,19},{4,20},{5,21},{6,22},{7,23},{8,24},{9,... | collective-permute-start | bytes 393224 | tf_op jit(solution)/shard_map/ppermute | solution.py:600
  104.0 1.2 collective-permute-start.28
  105.1 0.1 copy.20
  105.3 0.0 copy-start.3
  105.3 0.1 copy.21.edge_ref
  105.4 8.6 %collective-permute-done.27.refs_1_ = f32[64,512]{1,0:T(8,128)S(1)} collective-permute-done((f32[64,512]{1,0:T(8,128)S(1)}, f32[64,512]{1,0:T(8,128)S(1)}, u32[]{:S(2)}, u32[]{:S(2)}) %collective-permute-start.27) | collective-permute-done | bytes 131104 | tf_op jit(solution)/shard_map/ppermute | solution.py:600
  113.9 0.7 collective-permute-done.26.refs_2_
  114.6 0.8 shard_map.179
  115.4 4.0 %all-to-all-start.1 = ((f32[32,1,256]{2,1,0:T(1,128)}), f32[32,1,256]{2,1,0:T(1,128)S(1)}, u32[]{:S(2)}, u32[]{:S(2)}) async-start(f32[32,1,256]{2,1,0:T(1,128)} %get-tuple-element.234), calls=%async_computation.1 | async-start | bytes 65536 | tf_op jit(solution)/shard_map/all_to_all | solution.py:570
  119.4 7.2 %all-to-all-done.1.shared_ref = f32[32,1,256]{2,1,0:T(1,128)S(1)} async-done(((f32[32,1,256]{2,1,0:T(1,128)}), f32[32,1,256]{2,1,0:T(1,128)S(1)}, u32[]{:S(2)}, u32[]{:S(2)}) %all-to-all-start.1) | async-done | bytes 32800 | tf_op jit(solution)/shard_map/all_to_all | solution.py:570
  126.7 0.7 copy-done.5
  127.3 1.1 shard_map.180
  (84 shorter events, 0.3 us)
Async XLA Ops:
  0.6 0.7 copy-start.4
  2.3 19.5 %copy-start.10 = (f32[33,8,128]{2,1,0:T(8,128)}, f32[33,8,128]{2,1,0:T(8,128)S(1)}, u32[]{:S(2)}) copy-start(f32[33,8,128]{2,1,0:T(8,128)S(1)} %select_maximum_fusion.refs_0_) | copy-start | bytes 405508
  2.3 11.0 %copy-start.16 = (f32[3,2]{0,1:T(2,128)S(1)}, f32[3,2]{0,1:T(2,128)}, u32[]{:S(2)}) copy-start(f32[3,2]{0,1:T(2,128)} %param.11) | copy-start | bytes 76
  2.3 8.9 %collective-permute-start.5 = (f32[33,8,128]{2,1,0:T(8,128)S(1)}, f32[33,8,128]{2,1,0:T(8,128)S(1)}, u32[]{:S(2)}, u32[]{:S(2)}) collective-permute-start(f32[33,8,128]{2,1,0:T(8,128)S(1)} %select_maximum_fusion.refs_0_), channel_id=1, source_target_pairs={{0,8},{1,9},{2,10},{3,11},{4,12},{5,13},{6,14},{7,15},{8,0},{9,1},... | collective-permute-start | bytes 405512 | tf_op jit(solution)/shard_map/ppermute | solution.py:466
  5.4 13.2 %collective-permute-start.4 = (f32[33,8,128]{2,1,0:T(8,128)S(1)}, f32[33,8,128]{2,1,0:T(8,128)S(1)}, u32[]{:S(2)}, u32[]{:S(2)}) collective-permute-start(f32[33,8,128]{2,1,0:T(8,128)S(1)} %select_maximum_fusion.refs_0_), channel_id=1, source_target_pairs={{0,16},{1,17},{2,18},{3,19},{4,20},{5,21},{6,22},{7,23},{8,24},{9,... | collective-permute-start | bytes 405512 | tf_op jit(solution)/shard_map/ppermute | solution.py:466
  8.0 10.6 %collective-permute-start.3 = (f32[33,8,128]{2,1,0:T(8,128)S(1)}, f32[33,8,128]{2,1,0:T(8,128)S(1)}, u32[]{:S(2)}, u32[]{:S(2)}) collective-permute-start(f32[33,8,128]{2,1,0:T(8,128)S(1)} %select_maximum_fusion.refs_0_), channel_id=1, source_target_pairs={{0,24},{1,25},{2,26},{3,27},{4,28},{5,29},{6,30},{7,31},{8,16},{9,... | collective-permute-start | bytes 405512 | tf_op jit(solution)/shard_map/ppermute | solution.py:466
  8.0 10.6 %collective-permute-start.2 = (f32[33,8,128]{2,1,0:T(8,128)S(1)}, f32[33,8,128]{2,1,0:T(8,128)S(1)}, u32[]{:S(2)}, u32[]{:S(2)}) collective-permute-start(f32[33,8,128]{2,1,0:T(8,128)S(1)} %select_maximum_fusion.refs_0_), channel_id=1, source_target_pairs={{0,4},{1,5},{2,6},{3,7},{4,0},{5,1},{6,2},{7,3},{8,12},{9,13},{10,... | collective-permute-start | bytes 405512 | tf_op jit(solution)/shard_map/ppermute | solution.py:466
  9.8 8.9 %collective-permute-start.1 = (f32[33,8,128]{2,1,0:T(8,128)S(1)}, f32[33,8,128]{2,1,0:T(8,128)S(1)}, u32[]{:S(2)}, u32[]{:S(2)}) collective-permute-start(f32[33,8,128]{2,1,0:T(8,128)S(1)} %select_maximum_fusion.refs_0_), channel_id=1, source_target_pairs={{0,2},{1,3},{2,0},{3,1},{4,6},{5,7},{6,4},{7,5},{8,10},{9,11},{10,... | collective-permute-start | bytes 405512 | tf_op jit(solution)/shard_map/ppermute | solution.py:466
  11.3 7.4 %collective-permute-start = (f32[33,8,128]{2,1,0:T(8,128)S(1)}, f32[33,8,128]{2,1,0:T(8,128)S(1)}, u32[]{:S(2)}, u32[]{:S(2)}) collective-permute-start(f32[33,8,128]{2,1,0:T(8,128)S(1)} %select_maximum_fusion.refs_0_), channel_id=1, source_target_pairs={{0,6},{1,7},{2,4},{3,5},{4,2},{5,3},{6,0},{7,1},{8,14},{9,15},{10,... | collective-permute-start | bytes 405512 | tf_op jit(solution)/shard_map/ppermute | solution.py:466
  18.6 3.7 %copy-start.24 = (f32[33,8,128]{2,1,0:T(8,128)}, f32[33,8,128]{2,1,0:T(8,128)S(1)}, u32[]{:S(2)}) copy-start(f32[33,8,128]{2,1,0:T(8,128)S(1)} %collective-permute-done.2.refs_2_) | copy-start | bytes 405508
  18.7 3.2 %copy-start.25 = (f32[33,8,128]{2,1,0:T(8,128)}, f32[33,8,128]{2,1,0:T(8,128)S(1)}, u32[]{:S(2)}) copy-start(f32[33,8,128]{2,1,0:T(8,128)S(1)} %collective-permute-done.1.refs_1_) | copy-start | bytes 405508
  18.7 17.7 %copy-start.26 = (f32[33,8,128]{2,1,0:T(8,128)}, f32[33,8,128]{2,1,0:T(8,128)S(1)}, u32[]{:S(2)}) copy-start(f32[33,8,128]{2,1,0:T(8,128)S(1)} %collective-permute-done.refs_3_) | copy-start | bytes 405508
  18.7 20.9 %copy-start.14 = (f32[99,8,128]{2,1,0:T(8,128)}, f32[99,8,128]{2,1,0:T(8,128)S(1)}, u32[]{:S(2)}) copy-start(f32[99,8,128]{2,1,0:T(8,128)S(1)} %constant_dynamic-update-slice_fusion.refs_4_) | copy-start | bytes 1216516
  18.8 8.9 %collective-permute-start.10 = (f32[99,8,128]{2,1,0:T(8,128)S(1)}, f32[99,8,128]{2,1,0:T(8,128)S(1)}, u32[]{:S(2)}, u32[]{:S(2)}) collective-permute-start(f32[99,8,128]{2,1,0:T(8,128)S(1)} %constant_dynamic-update-slice_fusion.refs_4_), channel_id=1, source_target_pairs={{0,4},{1,5},{2,6},{3,7},{4,0},{5,1},{6,2},{7,3},{8,12},{9,13},{10,... | collective-permute-start | bytes 1216520 | tf_op jit(solution)/shard_map/ppermute | solution.py:466
  20.3 8.4 %collective-permute-start.9 = (f32[99,8,128]{2,1,0:T(8,128)S(1)}, f32[99,8,128]{2,1,0:T(8,128)S(1)}, u32[]{:S(2)}, u32[]{:S(2)}) collective-permute-start(f32[99,8,128]{2,1,0:T(8,128)S(1)} %constant_dynamic-update-slice_fusion.refs_4_), channel_id=1, source_target_pairs={{0,2},{1,3},{2,0},{3,1},{4,6},{5,7},{6,4},{7,5},{8,10},{9,11},{10,... | collective-permute-start | bytes 1216520 | tf_op jit(solution)/shard_map/ppermute | solution.py:466
  21.8 6.9 %collective-permute-start.8 = (f32[33,8,128]{2,1,0:T(8,128)S(1)}, f32[33,8,128]{2,1,0:T(8,128)S(1)}, u32[]{:S(2)}, u32[]{:S(2)}) collective-permute-start(f32[33,8,128]{2,1,0:T(8,128)S(1)} %select_maximum_fusion.refs_0_), channel_id=1, source_target_pairs={{0,1},{1,0},{2,3},{3,2},{4,5},{5,4},{6,7},{7,6},{8,9},{9,8},{10,11... | collective-permute-start | bytes 405512 | tf_op jit(solution)/shard_map/ppermute | solution.py:466
  21.8 6.9 %collective-permute-start.7 = (f32[33,8,128]{2,1,0:T(8,128)S(1)}, f32[33,8,128]{2,1,0:T(8,128)S(1)}, u32[]{:S(2)}, u32[]{:S(2)}) collective-permute-start(f32[33,8,128]{2,1,0:T(8,128)S(1)} %collective-permute-done.1.refs_1_), channel_id=1, source_target_pairs={{0,1},{1,0},{2,3},{3,2},{4,5},{5,4},{6,7},{7,6},{8,9},{9,8},{10,11... | collective-permute-start | bytes 405512 | tf_op jit(solution)/shard_map/ppermute | solution.py:466
  22.3 6.4 %collective-permute-start.6 = (f32[33,8,128]{2,1,0:T(8,128)S(1)}, f32[33,8,128]{2,1,0:T(8,128)S(1)}, u32[]{:S(2)}, u32[]{:S(2)}) collective-permute-start(f32[33,8,128]{2,1,0:T(8,128)S(1)} %collective-permute-done.2.refs_2_), channel_id=1, source_target_pairs={{0,1},{1,0},{2,3},{3,2},{4,5},{5,4},{6,7},{7,6},{8,9},{9,8},{10,11... | collective-permute-start | bytes 405512 | tf_op jit(solution)/shard_map/ppermute | solution.py:466
  27.7 3.3 %copy-start.12 = (f32[99,8,128]{2,1,0:T(8,128)}, f32[99,8,128]{2,1,0:T(8,128)S(1)}, u32[]{:S(2)}) copy-start(f32[99,8,128]{2,1,0:T(8,128)S(1)} %collective-permute-done.10.refs_6_) | copy-start | bytes 1216516
  27.7 10.2 %collective-permute-start.13 = (f32[99,8,128]{2,1,0:T(8,128)S(1)}, f32[99,8,128]{2,1,0:T(8,128)S(1)}, u32[]{:S(2)}, u32[]{:S(2)}) collective-permute-start(f32[99,8,128]{2,1,0:T(8,128)S(1)} %constant_dynamic-update-slice_fusion.refs_4_), channel_id=1, source_target_pairs={{0,1},{1,0},{2,3},{3,2},{4,5},{5,4},{6,7},{7,6},{8,9},{9,8},{10,11... | collective-permute-start | bytes 1216520 | tf_op jit(solution)/shard_map/ppermute | solution.py:466
  28.7 2.2 %copy-start.11 = (f32[99,8,128]{2,1,0:T(8,128)}, f32[99,8,128]{2,1,0:T(8,128)S(1)}, u32[]{:S(2)}) copy-start(f32[99,8,128]{2,1,0:T(8,128)S(1)} %collective-permute-done.9.refs_5_) | copy-start | bytes 1216516
  28.7 2.2 %copy-start.27 = (f32[33,8,128]{2,1,0:T(8,128)}, f32[33,8,128]{2,1,0:T(8,128)S(1)}, u32[]{:S(2)}) copy-start(f32[33,8,128]{2,1,0:T(8,128)S(1)} %collective-permute-done.8.refs_9_) | copy-start | bytes 405508
  28.7 2.2 %copy-start.28 = (f32[33,8,128]{2,1,0:T(8,128)}, f32[33,8,128]{2,1,0:T(8,128)S(1)}, u32[]{:S(2)}) copy-start(f32[33,8,128]{2,1,0:T(8,128)S(1)} %collective-permute-done.7.refs_10_) | copy-start | bytes 405508
  28.7 2.2 %copy-start.29 = (f32[33,8,128]{2,1,0:T(8,128)}, f32[33,8,128]{2,1,0:T(8,128)S(1)}, u32[]{:S(2)}) copy-start(f32[33,8,128]{2,1,0:T(8,128)S(1)} %collective-permute-done.6.refs_11_) | copy-start | bytes 405508
  28.7 9.1 %collective-permute-start.12 = (f32[99,8,128]{2,1,0:T(8,128)S(1)}, f32[99,8,128]{2,1,0:T(8,128)S(1)}, u32[]{:S(2)}, u32[]{:S(2)}) collective-permute-start(f32[99,8,128]{2,1,0:T(8,128)S(1)} %collective-permute-done.9.refs_5_), channel_id=1, source_target_pairs={{0,1},{1,0},{2,3},{3,2},{4,5},{5,4},{6,7},{7,6},{8,9},{9,8},{10,11... | collective-permute-start | bytes 1216520 | tf_op jit(solution)/shard_map/ppermute | solution.py:466
  28.8 9.0 %collective-permute-start.11 = (f32[99,8,128]{2,1,0:T(8,128)S(1)}, f32[99,8,128]{2,1,0:T(8,128)S(1)}, u32[]{:S(2)}, u32[]{:S(2)}) collective-permute-start(f32[99,8,128]{2,1,0:T(8,128)S(1)} %collective-permute-done.10.refs_6_), channel_id=1, source_target_pairs={{0,1},{1,0},{2,3},{3,2},{4,5},{5,4},{6,7},{7,6},{8,9},{9,8},{10,11... | collective-permute-start | bytes 1216520 | tf_op jit(solution)/shard_map/ppermute | solution.py:466
  29.3 7.0 %collective-permute-start.16 = (f32[49,8,128]{2,1,0:T(8,128)S(1)}, f32[49,8,128]{2,1,0:T(8,128)S(1)}, u32[]{:S(2)}, u32[]{:S(2)}) collective-permute-start(f32[49,8,128]{2,1,0:T(8,128)S(1)} %slice.21), channel_id=1, source_target_pairs={{0,2},{1,3},{2,0},{3,1},{4,6},{5,7},{6,4},{7,5},{8,10},{9,11},{10,... | collective-permute-start | bytes 602120 | tf_op jit(solution)/shard_map/ppermute | solution.py:466
  31.0 6.8 %collective-permute-start.15 = (f32[50,8,128]{2,1,0:T(8,128)S(1)}, f32[50,8,128]{2,1,0:T(8,128)S(1)}, u32[]{:S(2)}, u32[]{:S(2)}) collective-permute-start(f32[50,8,128]{2,1,0:T(8,128)S(1)} %slice.16), channel_id=1, source_target_pairs={{0,4},{1,5},{2,6},{3,7},{4,0},{5,1},{6,2},{7,3},{8,12},{9,13},{10,... | collective-permute-start | bytes 614408 | tf_op jit(solution)/shard_map/ppermute | solution.py:466
  36.4 3.3 %copy-start.22 = (f32[49,8,128]{2,1,0:T(8,128)}, f32[49,8,128]{2,1,0:T(8,128)S(1)}, u32[]{:S(2)}) copy-start(f32[49,8,128]{2,1,0:T(8,128)S(1)} %collective-permute-done.16.refs_7_) | copy-start | bytes 602116
  36.4 1.4 %collective-permute-start.14 = (f32[33,8,128]{2,1,0:T(8,128)S(1)}, f32[33,8,128]{2,1,0:T(8,128)S(1)}, u32[]{:S(2)}, u32[]{:S(2)}) collective-permute-start(f32[33,8,128]{2,1,0:T(8,128)S(1)} %collective-permute-done.refs_3_), channel_id=1, source_target_pairs={{0,1},{1,0},{2,3},{3,2},{4,5},{5,4},{6,7},{7,6},{8,9},{9,8},{10,11... | collective-permute-start | bytes 405512 | tf_op jit(solution)/shard_map/ppermute | solution.py:466
  37.8 1.9 %copy-start.20 = (f32[50,8,128]{2,1,0:T(8,128)}, f32[50,8,128]{2,1,0:T(8,128)S(1)}, u32[]{:S(2)}) copy-start(f32[50,8,128]{2,1,0:T(8,128)S(1)} %collective-permute-done.15.refs_8_) | copy-start | bytes 614404
  37.8 1.9 %copy-start.30 = (f32[33,8,128]{2,1,0:T(8,128)}, f32[33,8,128]{2,1,0:T(8,128)S(1)}, u32[]{:S(2)}) copy-start(f32[33,8,128]{2,1,0:T(8,128)S(1)} %collective-permute-done.14.refs_12_) | copy-start | bytes 405508
  37.8 1.9 %copy-start.17 = (f32[99,8,128]{2,1,0:T(8,128)}, f32[99,8,128]{2,1,0:T(8,128)S(1)}, u32[]{:S(2)}) copy-start(f32[99,8,128]{2,1,0:T(8,128)S(1)} %collective-permute-done.13.refs_13_) | copy-start | bytes 1216516
  37.8 1.9 %copy-start.18 = (f32[99,8,128]{2,1,0:T(8,128)}, f32[99,8,128]{2,1,0:T(8,128)S(1)}, u32[]{:S(2)}) copy-start(f32[99,8,128]{2,1,0:T(8,128)S(1)} %collective-permute-done.12.refs_14_) | copy-start | bytes 1216516
  37.9 1.9 %copy-start.19 = (f32[99,8,128]{2,1,0:T(8,128)}, f32[99,8,128]{2,1,0:T(8,128)S(1)}, u32[]{:S(2)}) copy-start(f32[99,8,128]{2,1,0:T(8,128)S(1)} %collective-permute-done.11.refs_15_) | copy-start | bytes 1216516
  37.9 1.8 %collective-permute-start.18 = (f32[50,8,128]{2,1,0:T(8,128)S(1)}, f32[50,8,128]{2,1,0:T(8,128)S(1)}, u32[]{:S(2)}, u32[]{:S(2)}) collective-permute-start(f32[50,8,128]{2,1,0:T(8,128)S(1)} %collective-permute-done.15.refs_8_), channel_id=1, source_target_pairs={{0,1},{1,0},{2,3},{3,2},{4,5},{5,4},{6,7},{7,6},{8,9},{9,8},{10,11... | collective-permute-start | bytes 614408 | tf_op jit(solution)/shard_map/ppermute | solution.py:466
  38.0 1.7 %collective-permute-start.17 = (f32[49,8,128]{2,1,0:T(8,128)S(1)}, f32[49,8,128]{2,1,0:T(8,128)S(1)}, u32[]{:S(2)}, u32[]{:S(2)}) collective-permute-start(f32[49,8,128]{2,1,0:T(8,128)S(1)} %collective-permute-done.16.refs_7_), channel_id=1, source_target_pairs={{0,1},{1,0},{2,3},{3,2},{4,5},{5,4},{6,7},{7,6},{8,9},{9,8},{10,11... | collective-permute-start | bytes 602120 | tf_op jit(solution)/shard_map/ppermute | solution.py:466
  39.7 0.7 copy-start.23
  40.4 0.7 copy-start.21
  74.8 2.0 %collective-permute-start.23 = (f32[192,512]{1,0:T(8,128)}, f32[192,512]{1,0:T(8,128)S(1)}, u32[]{:S(2)}, u32[]{:S(2)}) collective-permute-start(f32[192,512]{1,0:T(8,128)} %get-tuple-element.218), channel_id=1, source_target_pairs={{0,1},{1,0},{2,3},{3,2},{4,5},{5,4},{6,7},{7,6},{8,9},{9,8},{10,11... | collective-permute-start | bytes 1179656 | tf_op jit(solution)/shard_map/ppermute | solution.py:466
  75.1 4.5 %collective-permute-start.21 = (f32[192,512]{1,0:T(8,128)}, f32[192,512]{1,0:T(8,128)S(1)}, u32[]{:S(2)}, u32[]{:S(2)}) collective-permute-start(f32[192,512]{1,0:T(8,128)} %get-tuple-element.216), channel_id=1, source_target_pairs={{0,1},{1,0},{2,3},{3,2},{4,5},{5,4},{6,7},{7,6},{8,9},{9,8},{10,11... | collective-permute-start | bytes 1179656 | tf_op jit(solution)/shard_map/ppermute | solution.py:466
  75.4 5.6 %collective-permute-start.19 = (f32[192,512]{1,0:T(8,128)}, f32[192,512]{1,0:T(8,128)S(1)}, u32[]{:S(2)}, u32[]{:S(2)}) collective-permute-start(f32[192,512]{1,0:T(8,128)} %get-tuple-element.214), channel_id=1, source_target_pairs={{0,1},{1,0},{2,3},{3,2},{4,5},{5,4},{6,7},{7,6},{8,9},{9,8},{10,11... | collective-permute-start | bytes 1179656 | tf_op jit(solution)/shard_map/ppermute | solution.py:466
  75.6 13.8 %collective-permute-start.25 = (f32[192,512]{1,0:T(8,128)}, f32[192,512]{1,0:T(8,128)S(1)}, u32[]{:S(2)}, u32[]{:S(2)}) collective-permute-start(f32[192,512]{1,0:T(8,128)} %get-tuple-element.228), channel_id=1, source_target_pairs={{0,1},{1,0},{2,3},{3,2},{4,5},{5,4},{6,7},{7,6},{8,9},{9,8},{10,11... | collective-permute-start | bytes 1179656 | tf_op jit(solution)/shard_map/ppermute | solution.py:466
  76.8 2.7 %copy-start.9 = (f32[192,512]{1,0:T(8,128)S(1)}, f32[192,512]{1,0:T(8,128)}, u32[]{:S(2)}) copy-start(f32[192,512]{1,0:T(8,128)} %get-tuple-element.215) | copy-start | bytes 1179652
  77.9 13.0 %collective-permute-start.24 = (f32[192,512]{1,0:T(8,128)S(1)}, f32[192,512]{1,0:T(8,128)S(1)}, u32[]{:S(2)}, u32[]{:S(2)}) collective-permute-start(f32[192,512]{1,0:T(8,128)S(1)} %add.100), channel_id=1, source_target_pairs={{0,6},{1,7},{2,4},{3,5},{4,2},{5,3},{6,0},{7,1},{8,14},{9,15},{10,... | collective-permute-start | bytes 1179656 | tf_op jit(solution)/shard_map/ppermute | solution.py:466
  79.5 1.4 %copy-start.8 = (f32[192,512]{1,0:T(8,128)S(1)}, f32[192,512]{1,0:T(8,128)}, u32[]{:S(2)}) copy-start(f32[192,512]{1,0:T(8,128)} %get-tuple-element.213) | copy-start | bytes 1179652
  79.6 19.4 %collective-permute-start.22 = (f32[192,512]{1,0:T(8,128)S(1)}, f32[192,512]{1,0:T(8,128)S(1)}, u32[]{:S(2)}, u32[]{:S(2)}) collective-permute-start(f32[192,512]{1,0:T(8,128)S(1)} %add.99), channel_id=1, source_target_pairs={{0,4},{1,5},{2,6},{3,7},{4,0},{5,1},{6,2},{7,3},{8,12},{9,13},{10,... | collective-permute-start | bytes 1179656 | tf_op jit(solution)/shard_map/ppermute | solution.py:466
  81.0 1.4 %copy-start.13 = (f32[24,512]{1,0:T(8,128)S(1)}, f32[24,512]{1,0:T(8,128)}, u32[]{:S(2)}) copy-start(f32[24,512]{1,0:T(8,128)} %get-tuple-element.222) | copy-start | bytes 147460
  81.8 7.6 %copy-start.7 = (f32[192,512]{1,0:T(8,128)S(1)}, f32[192,512]{1,0:T(8,128)}, u32[]{:S(2)}) copy-start(f32[192,512]{1,0:T(8,128)} %get-tuple-element.227) | copy-start | bytes 1179652
  81.8 17.2 %collective-permute-start.20 = (f32[192,512]{1,0:T(8,128)}, f32[192,512]{1,0:T(8,128)S(1)}, u32[]{:S(2)}, u32[]{:S(2)}) collective-permute-start(f32[192,512]{1,0:T(8,128)} %add.98), channel_id=1, source_target_pairs={{0,2},{1,3},{2,0},{3,1},{4,6},{5,7},{6,4},{7,5},{8,10},{9,11},{10,... | collective-permute-start | bytes 1179656 | tf_op jit(solution)/shard_map/ppermute | solution.py:466
  83.3 15.8 %all-to-all-start = ((f32[32,1,320]{2,1,0:T(1,128)}), f32[32,1,320]{2,1,0:T(1,128)S(1)}, u32[]{:S(2)}, u32[]{:S(2)}) async-start(f32[32,1,320]{2,1,0:T(1,128)} %pad_maximum_fusion), calls=%async_computation | async-start | bytes 98304 | tf_op jit(solution)/shard_map/all_to_all | solution.py:570
  99.3 5.8 %copy-start.15 = (f32[16,512]{1,0:T(8,128)S(1)}, f32[16,512]{1,0:T(8,128)}, u32[]{:S(2)}) copy-start(f32[16,512]{1,0:T(8,128)} %get-tuple-element.235) | copy-start | bytes 98308
  99.3 14.6 %collective-permute-start.27 = (f32[64,512]{1,0:T(8,128)S(1)}, f32[64,512]{1,0:T(8,128)S(1)}, u32[]{:S(2)}, u32[]{:S(2)}) collective-permute-start(f32[64,512]{1,0:T(8,128)S(1)} %get-tuple-element.249), channel_id=1, source_target_pairs={{0,16},{1,17},{2,18},{3,19},{4,20},{5,21},{6,22},{7,23},{8,24},{9,... | collective-permute-start | bytes 393224 | tf_op jit(solution)/shard_map/ppermute | solution.py:600
  104.0 10.0 %collective-permute-start.28 = (f32[64,512]{1,0:T(8,128)S(1)}, f32[64,512]{1,0:T(8,128)S(1)}, u32[]{:S(2)}, u32[]{:S(2)}) collective-permute-start(f32[64,512]{1,0:T(8,128)S(1)} %get-tuple-element.248), channel_id=1, source_target_pairs={{0,24},{1,25},{2,26},{3,27},{4,28},{5,29},{6,30},{7,31},{8,16},{9,... | collective-permute-start | bytes 393224 | tf_op jit(solution)/shard_map/ppermute | solution.py:600
  105.1 9.5 %collective-permute-start.26 = (f32[64,512]{1,0:T(8,128)S(1)}, f32[64,512]{1,0:T(8,128)S(1)}, u32[]{:S(2)}, u32[]{:S(2)}) collective-permute-start(f32[64,512]{1,0:T(8,128)S(1)} %get-tuple-element.250), channel_id=1, source_target_pairs={{0,8},{1,9},{2,10},{3,11},{4,12},{5,13},{6,14},{7,15},{8,0},{9,1},... | collective-permute-start | bytes 393224 | tf_op jit(solution)/shard_map/ppermute | solution.py:600
  105.1 21.5 %copy-start.6 = (f32[192]{0:T(256)S(1)}, f32[192]{0:T(256)}, u32[]{:S(2)}) copy-start(f32[192]{0:T(256)} %param.21) | copy-start | bytes 2308
  105.3 9.4 %copy-start.3 = (s32[2,512]{1,0:T(2,128)S(1)}, s32[2,512]{1,0:T(2,128)}, u32[]{:S(2)}) copy-start(s32[2,512]{1,0:T(2,128)} %mask_ref.1) | copy-start | bytes 12292
  114.6 12.0 %copy-start.1 = (f32[64,512]{1,0:T(8,128)S(1)}, f32[64,512]{1,0:T(8,128)}, u32[]{:S(2)}) copy-start(f32[64,512]{1,0:T(8,128)} %refs_2_.1) | copy-start | bytes 393220
  114.6 12.0 %copy-start.2 = (f32[64,512]{1,0:T(8,128)S(1)}, f32[64,512]{1,0:T(8,128)}, u32[]{:S(2)}) copy-start(f32[64,512]{1,0:T(8,128)} %refs_3_.1) | copy-start | bytes 393220
  115.4 11.2 %copy-start = (f32[64,512]{1,0:T(8,128)S(1)}, f32[64,512]{1,0:T(8,128)}, u32[]{:S(2)}) copy-start(f32[64,512]{1,0:T(8,128)} %refs_1_.1) | copy-start | bytes 393220
  115.4 11.2 %all-to-all-start.1 = ((f32[32,1,256]{2,1,0:T(1,128)}), f32[32,1,256]{2,1,0:T(1,128)S(1)}, u32[]{:S(2)}, u32[]{:S(2)}) async-start(f32[32,1,256]{2,1,0:T(1,128)} %get-tuple-element.234), calls=%async_computation.1 | async-start | bytes 65536 | tf_op jit(solution)/shard_map/all_to_all | solution.py:570
  126.7 0.7 copy-start.5

commit v2 on v1

--- a/solution.py
+++ b/solution.py
@@ -27,6 +27,7 @@
 NN = (((1,), (0,)), ((), ()))
 NT = (((1,), (1,)), ((), ()))
 AXES = ("k", "b", "x", "c")
+PARTS = lambda lanes: 2 if lanes == 4 else 1
 FACTORS = 8 * D // 128
 
 
@@ -109,7 +110,8 @@
     if shared_edges:
         e_ref, refs = refs[0], refs[1:]
     pieces, refs = refs[: len(layout)], refs[len(layout) :]
-    aways, keeps, refs = refs[:lanes], refs[lanes : 2 * lanes], refs[2 * lanes :]
+    slots = lanes * PARTS(lanes)
+    aways, keeps, refs = refs[:slots], refs[slots : 2 * slots], refs[2 * slots :]
     small_ref, table_ref, dw_ref, full, left, et, limits, sums, wide, sems = refs[:10]
     wn, wt = refs[10:13], refs[13:16]
     rows = D // (2 * lanes)
@@ -386,12 +388,14 @@
             wide[at, 3 + j] = sum(points_of[j])
 
     copies = []
+    size = rows // PARTS(lanes)
     for half, refs in ((1 - core, aways), (core, keeps)):
-        for other in reversed(range(lanes)):
-            first = pl.multiple_of((2 * (lane ^ other) + half) * rows, 8)
-            for k in range(3):
-                there = refs[other].at[pl.ds(k * rows, rows)]
-                copies.append((dw_ref.at[k, pl.ds(first, rows)], there))
+        for part in range(rows // size):
+            for other in reversed(range(lanes)):
+                first = pl.multiple_of((2 * (lane ^ other) + half) * rows + part * size, 8)
+                for k in range(3):
+                    there = refs[part * lanes + other].at[pl.ds(k * size, size)]
+                    copies.append((dw_ref.at[k, pl.ds(first, size)], there))
     copies = start(copies)
 
     row = lax.broadcasted_iota(jnp.int32, (8, D), 0)
@@ -415,7 +419,8 @@
 
 def pair_grads(pairs, edges, pieces, layout, lanes):
     rows = D // (2 * lanes)
-    sent = [jax.ShapeDtypeStruct((3 * rows, D), F32)] * (2 * lanes)
+    slots = lanes * PARTS(lanes)
+    sent = [jax.ShapeDtypeStruct((3 * rows // PARTS(lanes), D), F32)] * (2 * slots)
     count = pairs[1].shape[1] * pairs[1].shape[2]
     segments = sum(len(one) for one in layout)
     vmem, held = pl.BlockSpec(memory_space=pltpu.VMEM), pl.BlockSpec(memory_space=pl.ANY)
@@ -433,7 +438,7 @@
             pltpu.VMEM((32, 128), F32),
             pltpu.VMEM((4, D, 128), F32),
             pltpu.VMEM((2, 7, D, 128), F32),
-            pltpu.SemaphoreType.DMA((max(segments, 6 * lanes),)),
+            pltpu.SemaphoreType.DMA((max(segments, 6 * slots),)),
         ]
         + [
             pltpu.VMEM((3, D, D), BF16),
@@ -446,7 +451,7 @@
             flops=54 * 2 * count * D * D, bytes_accessed=8 * 1024 * 1024, transcendentals=4 * count * D
         ),
     )(*pairs, *edges, *pieces)
-    return outs[:lanes], outs[lanes : 2 * lanes], *outs[2 * lanes :]
+    return outs[:slots], outs[slots : 2 * slots], *outs[2 * slots :]
 
 
 def adamw(weights, grads, first, second, rate):
@@ -580,25 +585,32 @@
     away, keep, small, edges = pair_grads(pairs, edges, pieces, layout, lanes)
 
     arrived = []
-    for other in reversed(range(lanes)):
-        part = keep[other] + exchange(away[other], 0, 0, 1, lanes)
-        arrived.append(exchange(part, 0, other, 0, lanes) if other else part)
-    arrived = [*in_turn(*arrived[:-1]), arrived[-1]]
+    for at in range(PARTS(lanes)):
+        got = []
+        for other in reversed(range(lanes)):
+            slot = at * lanes + other
+            part = keep[slot] + exchange(away[slot], 0, 0, 1, lanes)
+            got.append(exchange(part, 0, other, 0, lanes) if other else part)
+        arrived.append([*in_turn(*got[:-1]), got[-1]])
     shares = [small[:12].reshape(total, 1, share), small[16:24].reshape(FACTORS, 1, -1)]
     shares[1] = jnp.pad(shares[1], ((0, total - FACTORS), (0, 0), (0, 0)))
     shares = to_all(jnp.concatenate(shares, 2))
 
-    arrived[0], shares = lax.optimization_barrier((arrived[0], shares))
-
-    def rows_of(matrix):
-        at = jnp.maximum(matrix - 1, 0) * rows
-        return sum(lax.dynamic_slice_in_dim(one, at, rows, 0) for one in arrived)
-
+    arrived[-1][0], shares = lax.optimization_barrier((arrived[-1][0], shares))
     owned = []
-    for other in (3, 2, 1):
-        perm = [(i, i ^ (other * plane)) for i in range(total)]
-        owned.append(lax.ppermute(rows_of(which ^ other), AXES, perm))
-    owned = [*in_turn(*owned), rows_of(which)]
+    for terms in arrived:
+        size = rows // PARTS(lanes)
+
+        def rows_of(matrix):
+            at = jnp.maximum(matrix - 1, 0) * size
+            return sum(lax.dynamic_slice_in_dim(one, at, size, 0) for one in terms)
+
+        for other in (3, 2, 1):
+            perm = [(i, i ^ (other * plane)) for i in range(total)]
+            owned.append(lax.ppermute(rows_of(which ^ other), AXES, perm))
+        owned.append(rows_of(which))
+    ahead = in_turn(*(one for at, one in enumerate(owned) if at % 4 != 3))
+    owned = [x for at in range(0, len(ahead), 3) for x in (*ahead[at : at + 3], owned[at // 3 * 4 + 3])]
 
     kind = which.astype(jnp.int32).reshape(1)
     owned, own_edges, shared = collect(kind, owned, shares, pair_mask, share)
@@ -617,7 +629,11 @@
     share = edges_ref.shape[1]
     kind = kind_ref[0]
 
-    owned_ref[...] = jnp.where(kind == 0, 0.0, sum(one[...] for one in refs[:-3]))
+    terms = refs[:-3]
+    size = terms[0].shape[0]
+    for at in range(len(terms) // 4):
+        total = sum(one[...] for one in terms[4 * at : 4 * at + 4])
+        owned_ref[at * size : (at + 1) * size] = jnp.where(kind == 0, 0.0, total)
     shares = jnp.sum(shares_ref[...], 0)
     own = shares[:, :share]
     edges_ref[...] = own
@@ -634,7 +650,7 @@
 
 
 def collect(kind, owned, shares, mask, share):
-    rows, total = owned[0].shape[0], shares.shape[0]
+    rows, total = owned[0].shape[0] * (len(owned) // 4), shares.shape[0]
     smem, vmem = pl.BlockSpec(memory_space=pltpu.SMEM), pl.BlockSpec(memory_space=pltpu.VMEM)
     shapes = [(rows, D), (1, share), (total, 1, 256)]
     return pl.pallas_call(

time: 129 us -> 127 us (0.984)
  waiting for transfers between devices: 45.4 us -> 32.5 us
  starting transfers between devices: 38.4 us -> 47.1 us
  local copies, waits for them, and re-layouts: 3.8 us -> 6.56 us
    ppermute x26 -> x33, waiting for transfers between devices: 28.9 us -> 18.9 us  [exchange(): return lax.ppermute(x, AXES, [(i, i ^ mask) for i in range(total)])]
    ppermute x26 -> x33, starting transfers between devices: 22.6 us -> 27.8 us  [exchange(): return lax.ppermute(x, AXES, [(i, i ^ mask) for i in range(total)])]
    ppermute x3 -> x6, waiting for transfers between devices: 9.26 us -> 4.44 us  [local(): owned.append(lax.ppermute(rows_of(which ^ other), AXES, perm))]
    ppermute x3 -> x6, starting transfers between devices: 5.79 us -> 8.71 us  [local(): owned.append(lax.ppermute(rows_of(which ^ other), AXES, perm))]
    unnamed x64 -> x74, local copies, waits for them, and re-layouts: 2.75 us -> 5.51 us
    all_to_all x2, waiting for transfers between devices: 7.33 us -> 9.2 us  [to_all(): return lax.all_to_all(x, AXES, 0, 0, tiled=True)]
  transfers between devices with their start and end apart: 31 -> 41, of which waited for: 13 -> 11; matrix products, arithmetic and copies ran while one was open for 3% -> 3% of each run, Pallas kernels for 0% -> 0%
where the time goes in v2:
time: 127 us; the launch traced here: 126 us
  starting transfers between devices  47.1 us (37%)
  Pallas kernels  35.8 us (28%)
  waiting for transfers between devices  32.5 us (26%)
  local copies, waits for them, and re-layouts  6.56 us (5%)
  other arithmetic  3.16 us (2%)
  between operations  1.36 us (1%)
    pallas_call x1, Pallas kernels, pair_grads(): pl.pallas_call(functools.partial(pair_kernel, layout, lanes), in_specs=[v...  33.8 us
    ppermute x33, starting transfers between devices, exchange(): return lax.ppermute(x, AXES, [(i, i ^ mask) for i in range(total)])  27.8 us
    ppermute x33, waiting for transfers between devices, exchange(): return lax.ppermute(x, AXES, [(i, i ^ mask) for i in range(total)])  18.9 us
    all_to_all x2, starting transfers between devices, to_all(): return lax.all_to_all(x, AXES, 0, 0, tiled=True)  10.6 us
    all_to_all x2, waiting for transfers between devices, to_all(): return lax.all_to_all(x, AXES, 0, 0, tiled=True)  9.2 us
    ppermute x6, starting transfers between devices, local(): owned.append(lax.ppermute(rows_of(which ^ other), AXES, perm))  8.71 us
    unnamed x74, local copies, waits for them, and re-layouts  5.51 us
    ppermute x6, waiting for transfers between devices, local(): owned.append(lax.ppermute(rows_of(which ^ other), AXES, perm))  4.44 us
  transfers between devices with their start and end apart: 41, of which 11 were waited for; matrix products, arithmetic and copies ran while one was open for 3% of the time, Pallas kernels for 0%

profile of v2, /device:TPU:0, one launch (start us, length us, event | category | flops | bytes accessed | tf_op | source)
XLA Modules:
  0.0 126.5 jit_solution(14494087145711814674)
XLA Ops:
  0.7 0.7 copy-done.4
  1.4 0.9 select_maximum_fusion.refs_0_
  2.3 3.1 %collective-permute-start.5 = (f32[33,8,128]{2,1,0:T(8,128)S(1)}, f32[33,8,128]{2,1,0:T(8,128)S(1)}, u32[]{:S(2)}, u32[]{:S(2)}) collective-permute-start(f32[33,8,128]{2,1,0:T(8,128)S(1)} %select_maximum_fusion.refs_0_), channel_id=1, source_target_pairs={{0,8},{1,9},{2,10},{3,11},{4,12},{5,13},{6,14},{7,15},{8,0},{9,1},... | collective-permute-start | bytes 405512 | tf_op jit(solution)/shard_map/ppermute | solution.py:471
  5.4 2.6 %collective-permute-start.4 = (f32[33,8,128]{2,1,0:T(8,128)S(1)}, f32[33,8,128]{2,1,0:T(8,128)S(1)}, u32[]{:S(2)}, u32[]{:S(2)}) collective-permute-start(f32[33,8,128]{2,1,0:T(8,128)S(1)} %select_maximum_fusion.refs_0_), channel_id=1, source_target_pairs={{0,16},{1,17},{2,18},{3,19},{4,20},{5,21},{6,22},{7,23},{8,24},{9,... | collective-permute-start | bytes 405512 | tf_op jit(solution)/shard_map/ppermute | solution.py:471
  8.0 1.7 %collective-permute-start.2 = (f32[33,8,128]{2,1,0:T(8,128)S(1)}, f32[33,8,128]{2,1,0:T(8,128)S(1)}, u32[]{:S(2)}, u32[]{:S(2)}) collective-permute-start(f32[33,8,128]{2,1,0:T(8,128)S(1)} %select_maximum_fusion.refs_0_), channel_id=1, source_target_pairs={{0,4},{1,5},{2,6},{3,7},{4,0},{5,1},{6,2},{7,3},{8,12},{9,13},{10,... | collective-permute-start | bytes 405512 | tf_op jit(solution)/shard_map/ppermute | solution.py:471
  9.8 1.5 %collective-permute-start.1 = (f32[33,8,128]{2,1,0:T(8,128)S(1)}, f32[33,8,128]{2,1,0:T(8,128)S(1)}, u32[]{:S(2)}, u32[]{:S(2)}) collective-permute-start(f32[33,8,128]{2,1,0:T(8,128)S(1)} %select_maximum_fusion.refs_0_), channel_id=1, source_target_pairs={{0,2},{1,3},{2,0},{3,1},{4,6},{5,7},{6,4},{7,5},{8,10},{9,11},{10,... | collective-permute-start | bytes 405512 | tf_op jit(solution)/shard_map/ppermute | solution.py:471
  11.3 2.1 %collective-permute-start = (f32[33,8,128]{2,1,0:T(8,128)S(1)}, f32[33,8,128]{2,1,0:T(8,128)S(1)}, u32[]{:S(2)}, u32[]{:S(2)}) collective-permute-start(f32[33,8,128]{2,1,0:T(8,128)S(1)} %select_maximum_fusion.refs_0_), channel_id=1, source_target_pairs={{0,6},{1,7},{2,4},{3,5},{4,2},{5,3},{6,0},{7,1},{8,14},{9,15},{10,... | collective-permute-start | bytes 405512 | tf_op jit(solution)/shard_map/ppermute | solution.py:471
  13.3 0.7 broadcast_in_dim.14.src_ref
  14.0 4.6 %collective-permute-done.4 = f32[33,8,128]{2,1,0:T(8,128)S(1)} collective-permute-done((f32[33,8,128]{2,1,0:T(8,128)S(1)}, f32[33,8,128]{2,1,0:T(8,128)S(1)}, u32[]{:S(2)}, u32[]{:S(2)}) %collective-permute-start.4) | collective-permute-done | bytes 135200 | tf_op jit(solution)/shard_map/ppermute | solution.py:471
  18.8 1.6 %collective-permute-start.10 = (f32[99,8,128]{2,1,0:T(8,128)S(1)}, f32[99,8,128]{2,1,0:T(8,128)S(1)}, u32[]{:S(2)}, u32[]{:S(2)}) collective-permute-start(f32[99,8,128]{2,1,0:T(8,128)S(1)} %constant_dynamic-update-slice_fusion.refs_4_), channel_id=1, source_target_pairs={{0,4},{1,5},{2,6},{3,7},{4,0},{5,1},{6,2},{7,3},{8,12},{9,13},{10,... | collective-permute-start | bytes 1216520 | tf_op jit(solution)/shard_map/ppermute | solution.py:471
  20.3 1.5 %collective-permute-start.9 = (f32[99,8,128]{2,1,0:T(8,128)S(1)}, f32[99,8,128]{2,1,0:T(8,128)S(1)}, u32[]{:S(2)}, u32[]{:S(2)}) collective-permute-start(f32[99,8,128]{2,1,0:T(8,128)S(1)} %constant_dynamic-update-slice_fusion.refs_4_), channel_id=1, source_target_pairs={{0,2},{1,3},{2,0},{3,1},{4,6},{5,7},{6,4},{7,5},{8,10},{9,11},{10,... | collective-permute-start | bytes 1216520 | tf_op jit(solution)/shard_map/ppermute | solution.py:471
  21.8 0.5 collective-permute-start.7
  22.4 5.2 %collective-permute-done.10.refs_6_ = f32[99,8,128]{2,1,0:T(8,128)S(1)} collective-permute-done((f32[99,8,128]{2,1,0:T(8,128)S(1)}, f32[99,8,128]{2,1,0:T(8,128)S(1)}, u32[]{:S(2)}, u32[]{:S(2)}) %collective-permute-start.10) | collective-permute-done | bytes 405536 | tf_op jit(solution)/shard_map/ppermute | solution.py:471
  27.7 1.0 collective-permute-done.9.refs_5_
  28.8 0.5 collective-permute-start.11
  29.3 1.6 %collective-permute-start.16 = (f32[49,8,128]{2,1,0:T(8,128)S(1)}, f32[49,8,128]{2,1,0:T(8,128)S(1)}, u32[]{:S(2)}, u32[]{:S(2)}) collective-permute-start(f32[49,8,128]{2,1,0:T(8,128)S(1)} %slice.21), channel_id=1, source_target_pairs={{0,2},{1,3},{2,0},{3,1},{4,6},{5,7},{6,4},{7,5},{8,10},{9,11},{10,... | collective-permute-start | bytes 602120 | tf_op jit(solution)/shard_map/ppermute | solution.py:471
  31.0 0.6 collective-permute-start.15
  31.5 4.8 %collective-permute-done.16.refs_7_ = f32[49,8,128]{2,1,0:T(8,128)S(1)} collective-permute-done((f32[49,8,128]{2,1,0:T(8,128)S(1)}, f32[49,8,128]{2,1,0:T(8,128)S(1)}, u32[]{:S(2)}, u32[]{:S(2)}) %collective-permute-start.16) | collective-permute-done | bytes 200736 | tf_op jit(solution)/shard_map/ppermute | solution.py:471
  36.4 1.4 %collective-permute-done.15.refs_8_ = f32[50,8,128]{2,1,0:T(8,128)S(1)} collective-permute-done((f32[50,8,128]{2,1,0:T(8,128)S(1)}, f32[50,8,128]{2,1,0:T(8,128)S(1)}, u32[]{:S(2)}, u32[]{:S(2)}) %collective-permute-start.15) | collective-permute-done | bytes 204832 | tf_op jit(solution)/shard_map/ppermute | solution.py:471
  37.9 0.1 collective-permute-start.18
  38.0 0.5 collective-permute-start.17
  38.5 1.2 collective-permute-done.17.refs_16_
  39.8 0.6 copy-done.27
  40.4 0.7 copy-done.25
  41.0 33.8 %shard_map.178 = (f32[96,512]{1,0:T(8,128)}, f32[96,512]{1,0:T(8,128)}, f32[96,512]{1,0:T(8,128)}, f32[96,512]{1,0:T(8,128)}, f32[96,512]{1,0:T(8,128)}, /*index...) custom-call(f32[2,3,128]{2,1,0:T(4,128)} %broadcast_in_dim.14.src_re, ...), custom_call_target="tpu_custom_call" | custom-call | flops 28991029248 | bytes 8388608 | tf_op jit(solution)/shard_map/pallas_call | solution.py:427
  74.9 0.3 collective-permute-start.33
  75.2 0.3 collective-permute-start.31
  75.5 0.2 collective-permute-start.29
  75.7 0.3 collective-permute-start.23
  76.0 0.2 collective-permute-start.21
  76.2 0.4 collective-permute-done.33
  76.6 0.2 collective-permute-start.19
  76.8 1.0 add.180
  77.9 0.4 collective-permute-start.35
  78.2 0.2 collective-permute-start.25
  78.4 1.6 %collective-permute-start.34 = (f32[96,512]{1,0:T(8,128)S(1)}, f32[96,512]{1,0:T(8,128)S(1)}, u32[]{:S(2)}, u32[]{:S(2)}) collective-permute-start(f32[96,512]{1,0:T(8,128)S(1)} %add.180), channel_id=1, source_target_pairs={{0,6},{1,7},{2,4},{3,5},{4,2},{5,3},{6,0},{7,1},{8,14},{9,15},{10,... | collective-permute-start | bytes 589832 | tf_op jit(solution)/shard_map/ppermute | solution.py:471
  80.1 1.3 %collective-permute-start.32 = (f32[96,512]{1,0:T(8,128)S(1)}, f32[96,512]{1,0:T(8,128)S(1)}, u32[]{:S(2)}, u32[]{:S(2)}) collective-permute-start(f32[96,512]{1,0:T(8,128)S(1)} %add.179), channel_id=1, source_target_pairs={{0,4},{1,5},{2,6},{3,7},{4,0},{5,1},{6,2},{7,3},{8,12},{9,13},{10,... | collective-permute-start | bytes 589832 | tf_op jit(solution)/shard_map/ppermute | solution.py:471
  81.5 0.7 collective-permute-start.30
  82.2 0.1 reshape.45
  82.4 0.9 copy-done.10
  83.3 0.9 copy-done.9
  84.3 1.6 %collective-permute-start.24 = (f32[96,512]{1,0:T(8,128)S(1)}, f32[96,512]{1,0:T(8,128)S(1)}, u32[]{:S(2)}, u32[]{:S(2)}) collective-permute-start(f32[96,512]{1,0:T(8,128)S(1)} %add.164), channel_id=1, source_target_pairs={{0,6},{1,7},{2,4},{3,5},{4,2},{5,3},{6,0},{7,1},{8,14},{9,15},{10,... | collective-permute-start | bytes 589832 | tf_op jit(solution)/shard_map/ppermute | solution.py:471
  85.9 1.2 collective-permute-start.22
  87.2 1.3 %collective-permute-start.20 = (f32[96,512]{1,0:T(8,128)S(1)}, f32[96,512]{1,0:T(8,128)S(1)}, u32[]{:S(2)}, u32[]{:S(2)}) collective-permute-start(f32[96,512]{1,0:T(8,128)S(1)} %add.162), channel_id=1, source_target_pairs={{0,2},{1,3},{2,0},{3,1},{4,6},{5,7},{6,4},{7,5},{8,10},{9,11},{10,... | collective-permute-start | bytes 589832 | tf_op jit(solution)/shard_map/ppermute | solution.py:471
  88.5 0.8 pad_maximum_fusion
  89.3 5.3 %all-to-all-start = ((f32[32,1,320]{2,1,0:T(1,128)}), f32[32,1,320]{2,1,0:T(1,128)S(1)}, u32[]{:S(2)}, u32[]{:S(2)}) async-start(f32[32,1,320]{2,1,0:T(1,128)} %pad_maximum_fusion), calls=%async_computation | async-start | bytes 98304 | tf_op jit(solution)/shard_map/all_to_all | solution.py:575
  94.6 0.9 copy-done.7
  95.6 0.1 dynamic-slice_add_fusion.1
  95.7 2.7 %collective-permute-start.37 = (f32[32,512]{1,0:T(8,128)S(1)}, f32[32,512]{1,0:T(8,128)S(1)}, u32[]{:S(2)}, u32[]{:S(2)}) collective-permute-start(f32[32,512]{1,0:T(8,128)S(1)} %get-tuple-element.309), channel_id=1, source_target_pairs={{0,16},{1,17},{2,18},{3,19},{4,20},{5,21},{6,22},{7,23},{8,24},{9,... | collective-permute-start | bytes 196616 | tf_op jit(solution)/shard_map/ppermute | solution.py:610
  98.4 1.5 %collective-permute-start.38 = (f32[32,512]{1,0:T(8,128)S(1)}, f32[32,512]{1,0:T(8,128)S(1)}, u32[]{:S(2)}, u32[]{:S(2)}) collective-permute-start(f32[32,512]{1,0:T(8,128)S(1)} %get-tuple-element.308), channel_id=1, source_target_pairs={{0,24},{1,25},{2,26},{3,27},{4,28},{5,29},{6,30},{7,31},{8,16},{9,... | collective-permute-start | bytes 196616 | tf_op jit(solution)/shard_map/ppermute | solution.py:610
  99.9 2.0 %all-to-all-done.shares_ref = f32[32,1,320]{2,1,0:T(1,128)S(1)} async-done(((f32[32,1,320]{2,1,0:T(1,128)}), f32[32,1,320]{2,1,0:T(1,128)S(1)}, u32[]{:S(2)}, u32[]{:S(2)}) %all-to-all-start) | async-done | bytes 40992 | tf_op jit(solution)/shard_map/all_to_all | solution.py:575
  101.9 0.1 dynamic-slice_add_fusion
  102.0 1.7 %collective-permute-start.28 = (f32[32,512]{1,0:T(8,128)S(1)}, f32[32,512]{1,0:T(8,128)S(1)}, u32[]{:S(2)}, u32[]{:S(2)}) collective-permute-start(f32[32,512]{1,0:T(8,128)S(1)} %get-tuple-element.304), channel_id=1, source_target_pairs={{0,24},{1,25},{2,26},{3,27},{4,28},{5,29},{6,30},{7,31},{8,16},{9,... | collective-permute-start | bytes 196616 | tf_op jit(solution)/shard_map/ppermute | solution.py:610
  103.7 1.0 collective-permute-start.27
  104.7 1.8 %collective-permute-start.26 = (f32[32,512]{1,0:T(8,128)S(1)}, f32[32,512]{1,0:T(8,128)S(1)}, u32[]{:S(2)}, u32[]{:S(2)}) collective-permute-start(f32[32,512]{1,0:T(8,128)S(1)} %get-tuple-element.306), channel_id=1, source_target_pairs={{0,8},{1,9},{2,10},{3,11},{4,12},{5,13},{6,14},{7,15},{8,0},{9,1},... | collective-permute-start | bytes 196616 | tf_op jit(solution)/shard_map/ppermute | solution.py:610
  106.5 0.1 copy.20
  106.6 0.1 copy.21.edge_ref
  106.7 1.9 %collective-permute-done.28.refs_4_ = f32[32,512]{1,0:T(8,128)S(1)} collective-permute-done((f32[32,512]{1,0:T(8,128)S(1)}, f32[32,512]{1,0:T(8,128)S(1)}, u32[]{:S(2)}, u32[]{:S(2)}) %collective-permute-start.28) | collective-permute-done | bytes 65568 | tf_op jit(solution)/shard_map/ppermute | solution.py:610
  108.7 2.5 %collective-permute-done.27.refs_5_ = f32[32,512]{1,0:T(8,128)S(1)} collective-permute-done((f32[32,512]{1,0:T(8,128)S(1)}, f32[32,512]{1,0:T(8,128)S(1)}, u32[]{:S(2)}, u32[]{:S(2)}) %collective-permute-start.27) | collective-permute-done | bytes 65568 | tf_op jit(solution)/shard_map/ppermute | solution.py:610
  111.2 0.8 shard_map.179
  111.9 5.3 %all-to-all-start.1 = ((f32[32,1,256]{2,1,0:T(1,128)}), f32[32,1,256]{2,1,0:T(1,128)S(1)}, u32[]{:S(2)}, u32[]{:S(2)}) async-start(f32[32,1,256]{2,1,0:T(1,128)} %get-tuple-element.290), calls=%async_computation.1 | async-start | bytes 65536 | tf_op jit(solution)/shard_map/all_to_all | solution.py:575
  117.3 7.2 %all-to-all-done.1.shared_ref = f32[32,1,256]{2,1,0:T(1,128)S(1)} async-done(((f32[32,1,256]{2,1,0:T(1,128)}), f32[32,1,256]{2,1,0:T(1,128)S(1)}, u32[]{:S(2)}, u32[]{:S(2)}) %all-to-all-start.1) | async-done | bytes 32800 | tf_op jit(solution)/shard_map/all_to_all | solution.py:575
  124.5 0.7 copy-done.5
  125.2 1.1 shard_map.180
  (119 shorter events, 0.9 us)
Async XLA Ops:
  2.3 19.5 %copy-start.14 = (f32[33,8,128]{2,1,0:T(8,128)}, f32[33,8,128]{2,1,0:T(8,128)S(1)}, u32[]{:S(2)}) copy-start(f32[33,8,128]{2,1,0:T(8,128)S(1)} %select_maximum_fusion.refs_0_) | copy-start | bytes 405508
  2.3 11.0 %copy-start.20 = (f32[3,2]{0,1:T(2,128)S(1)}, f32[3,2]{0,1:T(2,128)}, u32[]{:S(2)}) copy-start(f32[3,2]{0,1:T(2,128)} %param.11) | copy-start | bytes 76
  2.3 8.9 %collective-permute-start.5 = (f32[33,8,128]{2,1,0:T(8,128)S(1)}, f32[33,8,128]{2,1,0:T(8,128)S(1)}, u32[]{:S(2)}, u32[]{:S(2)}) collective-permute-start(f32[33,8,128]{2,1,0:T(8,128)S(1)} %select_maximum_fusion.refs_0_), channel_id=1, source_target_pairs={{0,8},{1,9},{2,10},{3,11},{4,12},{5,13},{6,14},{7,15},{8,0},{9,1},... | collective-permute-start | bytes 405512 | tf_op jit(solution)/shard_map/ppermute | solution.py:471
  5.4 13.2 %collective-permute-start.4 = (f32[33,8,128]{2,1,0:T(8,128)S(1)}, f32[33,8,128]{2,1,0:T(8,128)S(1)}, u32[]{:S(2)}, u32[]{:S(2)}) collective-permute-start(f32[33,8,128]{2,1,0:T(8,128)S(1)} %select_maximum_fusion.refs_0_), channel_id=1, source_target_pairs={{0,16},{1,17},{2,18},{3,19},{4,20},{5,21},{6,22},{7,23},{8,24},{9,... | collective-permute-start | bytes 405512 | tf_op jit(solution)/shard_map/ppermute | solution.py:471
  8.0 10.6 %collective-permute-start.3 = (f32[33,8,128]{2,1,0:T(8,128)S(1)}, f32[33,8,128]{2,1,0:T(8,128)S(1)}, u32[]{:S(2)}, u32[]{:S(2)}) collective-permute-start(f32[33,8,128]{2,1,0:T(8,128)S(1)} %select_maximum_fusion.refs_0_), channel_id=1, source_target_pairs={{0,24},{1,25},{2,26},{3,27},{4,28},{5,29},{6,30},{7,31},{8,16},{9,... | collective-permute-start | bytes 405512 | tf_op jit(solution)/shard_map/ppermute | solution.py:471
  8.0 10.6 %collective-permute-start.2 = (f32[33,8,128]{2,1,0:T(8,128)S(1)}, f32[33,8,128]{2,1,0:T(8,128)S(1)}, u32[]{:S(2)}, u32[]{:S(2)}) collective-permute-start(f32[33,8,128]{2,1,0:T(8,128)S(1)} %select_maximum_fusion.refs_0_), channel_id=1, source_target_pairs={{0,4},{1,5},{2,6},{3,7},{4,0},{5,1},{6,2},{7,3},{8,12},{9,13},{10,... | collective-permute-start | bytes 405512 | tf_op jit(solution)/shard_map/ppermute | solution.py:471
  9.8 8.9 %collective-permute-start.1 = (f32[33,8,128]{2,1,0:T(8,128)S(1)}, f32[33,8,128]{2,1,0:T(8,128)S(1)}, u32[]{:S(2)}, u32[]{:S(2)}) collective-permute-start(f32[33,8,128]{2,1,0:T(8,128)S(1)} %select_maximum_fusion.refs_0_), channel_id=1, source_target_pairs={{0,2},{1,3},{2,0},{3,1},{4,6},{5,7},{6,4},{7,5},{8,10},{9,11},{10,... | collective-permute-start | bytes 405512 | tf_op jit(solution)/shard_map/ppermute | solution.py:471
  11.3 7.4 %collective-permute-start = (f32[33,8,128]{2,1,0:T(8,128)S(1)}, f32[33,8,128]{2,1,0:T(8,128)S(1)}, u32[]{:S(2)}, u32[]{:S(2)}) collective-permute-start(f32[33,8,128]{2,1,0:T(8,128)S(1)} %select_maximum_fusion.refs_0_), channel_id=1, source_target_pairs={{0,6},{1,7},{2,4},{3,5},{4,2},{5,3},{6,0},{7,1},{8,14},{9,15},{10,... | collective-permute-start | bytes 405512 | tf_op jit(solution)/shard_map/ppermute | solution.py:471
  18.6 3.7 %copy-start.29 = (f32[33,8,128]{2,1,0:T(8,128)}, f32[33,8,128]{2,1,0:T(8,128)S(1)}, u32[]{:S(2)}) copy-start(f32[33,8,128]{2,1,0:T(8,128)S(1)} %collective-permute-done.2.refs_2_) | copy-start | bytes 405508
  18.7 3.2 %copy-start.30 = (f32[33,8,128]{2,1,0:T(8,128)}, f32[33,8,128]{2,1,0:T(8,128)S(1)}, u32[]{:S(2)}) copy-start(f32[33,8,128]{2,1,0:T(8,128)S(1)} %collective-permute-done.1.refs_1_) | copy-start | bytes 405508
  18.7 17.7 %copy-start.31 = (f32[33,8,128]{2,1,0:T(8,128)}, f32[33,8,128]{2,1,0:T(8,128)S(1)}, u32[]{:S(2)}) copy-start(f32[33,8,128]{2,1,0:T(8,128)S(1)} %collective-permute-done.refs_3_) | copy-start | bytes 405508
  18.7 20.9 %copy-start.18 = (f32[99,8,128]{2,1,0:T(8,128)}, f32[99,8,128]{2,1,0:T(8,128)S(1)}, u32[]{:S(2)}) copy-start(f32[99,8,128]{2,1,0:T(8,128)S(1)} %constant_dynamic-update-slice_fusion.refs_4_) | copy-start | bytes 1216516
  18.8 8.9 %collective-permute-start.10 = (f32[99,8,128]{2,1,0:T(8,128)S(1)}, f32[99,8,128]{2,1,0:T(8,128)S(1)}, u32[]{:S(2)}, u32[]{:S(2)}) collective-permute-start(f32[99,8,128]{2,1,0:T(8,128)S(1)} %constant_dynamic-update-slice_fusion.refs_4_), channel_id=1, source_target_pairs={{0,4},{1,5},{2,6},{3,7},{4,0},{5,1},{6,2},{7,3},{8,12},{9,13},{10,... | collective-permute-start | bytes 1216520 | tf_op jit(solution)/shard_map/ppermute | solution.py:471
  20.3 8.4 %collective-permute-start.9 = (f32[99,8,128]{2,1,0:T(8,128)S(1)}, f32[99,8,128]{2,1,0:T(8,128)S(1)}, u32[]{:S(2)}, u32[]{:S(2)}) collective-permute-start(f32[99,8,128]{2,1,0:T(8,128)S(1)} %constant_dynamic-update-slice_fusion.refs_4_), channel_id=1, source_target_pairs={{0,2},{1,3},{2,0},{3,1},{4,6},{5,7},{6,4},{7,5},{8,10},{9,11},{10,... | collective-permute-start | bytes 1216520 | tf_op jit(solution)/shard_map/ppermute | solution.py:471
  21.8 6.9 %collective-permute-start.8 = (f32[33,8,128]{2,1,0:T(8,128)S(1)}, f32[33,8,128]{2,1,0:T(8,128)S(1)}, u32[]{:S(2)}, u32[]{:S(2)}) collective-permute-start(f32[33,8,128]{2,1,0:T(8,128)S(1)} %select_maximum_fusion.refs_0_), channel_id=1, source_target_pairs={{0,1},{1,0},{2,3},{3,2},{4,5},{5,4},{6,7},{7,6},{8,9},{9,8},{10,11... | collective-permute-start | bytes 405512 | tf_op jit(solution)/shard_map/ppermute | solution.py:471
  21.8 6.9 %collective-permute-start.7 = (f32[33,8,128]{2,1,0:T(8,128)S(1)}, f32[33,8,128]{2,1,0:T(8,128)S(1)}, u32[]{:S(2)}, u32[]{:S(2)}) collective-permute-start(f32[33,8,128]{2,1,0:T(8,128)S(1)} %collective-permute-done.1.refs_1_), channel_id=1, source_target_pairs={{0,1},{1,0},{2,3},{3,2},{4,5},{5,4},{6,7},{7,6},{8,9},{9,8},{10,11... | collective-permute-start | bytes 405512 | tf_op jit(solution)/shard_map/ppermute | solution.py:471
  22.3 6.4 %collective-permute-start.6 = (f32[33,8,128]{2,1,0:T(8,128)S(1)}, f32[33,8,128]{2,1,0:T(8,128)S(1)}, u32[]{:S(2)}, u32[]{:S(2)}) collective-permute-start(f32[33,8,128]{2,1,0:T(8,128)S(1)} %collective-permute-done.2.refs_2_), channel_id=1, source_target_pairs={{0,1},{1,0},{2,3},{3,2},{4,5},{5,4},{6,7},{7,6},{8,9},{9,8},{10,11... | collective-permute-start | bytes 405512 | tf_op jit(solution)/shard_map/ppermute | solution.py:471
  27.7 3.3 %copy-start.16 = (f32[99,8,128]{2,1,0:T(8,128)}, f32[99,8,128]{2,1,0:T(8,128)S(1)}, u32[]{:S(2)}) copy-start(f32[99,8,128]{2,1,0:T(8,128)S(1)} %collective-permute-done.10.refs_6_) | copy-start | bytes 1216516
  27.7 10.2 %collective-permute-start.13 = (f32[99,8,128]{2,1,0:T(8,128)S(1)}, f32[99,8,128]{2,1,0:T(8,128)S(1)}, u32[]{:S(2)}, u32[]{:S(2)}) collective-permute-start(f32[99,8,128]{2,1,0:T(8,128)S(1)} %constant_dynamic-update-slice_fusion.refs_4_), channel_id=1, source_target_pairs={{0,1},{1,0},{2,3},{3,2},{4,5},{5,4},{6,7},{7,6},{8,9},{9,8},{10,11... | collective-permute-start | bytes 1216520 | tf_op jit(solution)/shard_map/ppermute | solution.py:471
  28.7 2.2 %copy-start.15 = (f32[99,8,128]{2,1,0:T(8,128)}, f32[99,8,128]{2,1,0:T(8,128)S(1)}, u32[]{:S(2)}) copy-start(f32[99,8,128]{2,1,0:T(8,128)S(1)} %collective-permute-done.9.refs_5_) | copy-start | bytes 1216516
  28.7 2.2 %copy-start.32 = (f32[33,8,128]{2,1,0:T(8,128)}, f32[33,8,128]{2,1,0:T(8,128)S(1)}, u32[]{:S(2)}) copy-start(f32[33,8,128]{2,1,0:T(8,128)S(1)} %collective-permute-done.8.refs_9_) | copy-start | bytes 405508
  28.7 2.2 %copy-start.33 = (f32[33,8,128]{2,1,0:T(8,128)}, f32[33,8,128]{2,1,0:T(8,128)S(1)}, u32[]{:S(2)}) copy-start(f32[33,8,128]{2,1,0:T(8,128)S(1)} %collective-permute-done.7.refs_10_) | copy-start | bytes 405508
  28.7 2.2 %copy-start.34 = (f32[33,8,128]{2,1,0:T(8,128)}, f32[33,8,128]{2,1,0:T(8,128)S(1)}, u32[]{:S(2)}) copy-start(f32[33,8,128]{2,1,0:T(8,128)S(1)} %collective-permute-done.6.refs_11_) | copy-start | bytes 405508
  28.7 9.1 %collective-permute-start.12 = (f32[99,8,128]{2,1,0:T(8,128)S(1)}, f32[99,8,128]{2,1,0:T(8,128)S(1)}, u32[]{:S(2)}, u32[]{:S(2)}) collective-permute-start(f32[99,8,128]{2,1,0:T(8,128)S(1)} %collective-permute-done.9.refs_5_), channel_id=1, source_target_pairs={{0,1},{1,0},{2,3},{3,2},{4,5},{5,4},{6,7},{7,6},{8,9},{9,8},{10,11... | collective-permute-start | bytes 1216520 | tf_op jit(solution)/shard_map/ppermute | solution.py:471
  28.8 9.0 %collective-permute-start.11 = (f32[99,8,128]{2,1,0:T(8,128)S(1)}, f32[99,8,128]{2,1,0:T(8,128)S(1)}, u32[]{:S(2)}, u32[]{:S(2)}) collective-permute-start(f32[99,8,128]{2,1,0:T(8,128)S(1)} %collective-permute-done.10.refs_6_), channel_id=1, source_target_pairs={{0,1},{1,0},{2,3},{3,2},{4,5},{5,4},{6,7},{7,6},{8,9},{9,8},{10,11... | collective-permute-start | bytes 1216520 | tf_op jit(solution)/shard_map/ppermute | solution.py:471
  29.3 7.0 %collective-permute-start.16 = (f32[49,8,128]{2,1,0:T(8,128)S(1)}, f32[49,8,128]{2,1,0:T(8,128)S(1)}, u32[]{:S(2)}, u32[]{:S(2)}) collective-permute-start(f32[49,8,128]{2,1,0:T(8,128)S(1)} %slice.21), channel_id=1, source_target_pairs={{0,2},{1,3},{2,0},{3,1},{4,6},{5,7},{6,4},{7,5},{8,10},{9,11},{10,... | collective-permute-start | bytes 602120 | tf_op jit(solution)/shard_map/ppermute | solution.py:471
  31.0 6.8 %collective-permute-start.15 = (f32[50,8,128]{2,1,0:T(8,128)S(1)}, f32[50,8,128]{2,1,0:T(8,128)S(1)}, u32[]{:S(2)}, u32[]{:S(2)}) collective-permute-start(f32[50,8,128]{2,1,0:T(8,128)S(1)} %slice.16), channel_id=1, source_target_pairs={{0,4},{1,5},{2,6},{3,7},{4,0},{5,1},{6,2},{7,3},{8,12},{9,13},{10,... | collective-permute-start | bytes 614408 | tf_op jit(solution)/shard_map/ppermute | solution.py:471
  36.4 3.3 %copy-start.26 = (f32[49,8,128]{2,1,0:T(8,128)}, f32[49,8,128]{2,1,0:T(8,128)S(1)}, u32[]{:S(2)}) copy-start(f32[49,8,128]{2,1,0:T(8,128)S(1)} %collective-permute-done.16.refs_7_) | copy-start | bytes 602116
  36.4 1.4 %collective-permute-start.14 = (f32[33,8,128]{2,1,0:T(8,128)S(1)}, f32[33,8,128]{2,1,0:T(8,128)S(1)}, u32[]{:S(2)}, u32[]{:S(2)}) collective-permute-start(f32[33,8,128]{2,1,0:T(8,128)S(1)} %collective-permute-done.refs_3_), channel_id=1, source_target_pairs={{0,1},{1,0},{2,3},{3,2},{4,5},{5,4},{6,7},{7,6},{8,9},{9,8},{10,11... | collective-permute-start | bytes 405512 | tf_op jit(solution)/shard_map/ppermute | solution.py:471
  37.8 1.9 %copy-start.24 = (f32[50,8,128]{2,1,0:T(8,128)}, f32[50,8,128]{2,1,0:T(8,128)S(1)}, u32[]{:S(2)}) copy-start(f32[50,8,128]{2,1,0:T(8,128)S(1)} %collective-permute-done.15.refs_8_) | copy-start | bytes 614404
  37.8 1.9 %copy-start.35 = (f32[33,8,128]{2,1,0:T(8,128)}, f32[33,8,128]{2,1,0:T(8,128)S(1)}, u32[]{:S(2)}) copy-start(f32[33,8,128]{2,1,0:T(8,128)S(1)} %collective-permute-done.14.refs_12_) | copy-start | bytes 405508
  37.8 1.9 %copy-start.21 = (f32[99,8,128]{2,1,0:T(8,128)}, f32[99,8,128]{2,1,0:T(8,128)S(1)}, u32[]{:S(2)}) copy-start(f32[99,8,128]{2,1,0:T(8,128)S(1)} %collective-permute-done.13.refs_13_) | copy-start | bytes 1216516
  37.9 1.8 %collective-permute-start.18 = (f32[50,8,128]{2,1,0:T(8,128)S(1)}, f32[50,8,128]{2,1,0:T(8,128)S(1)}, u32[]{:S(2)}, u32[]{:S(2)}) collective-permute-start(f32[50,8,128]{2,1,0:T(8,128)S(1)} %collective-permute-done.15.refs_8_), channel_id=1, source_target_pairs={{0,1},{1,0},{2,3},{3,2},{4,5},{5,4},{6,7},{7,6},{8,9},{9,8},{10,11... | collective-permute-start | bytes 614408 | tf_op jit(solution)/shard_map/ppermute | solution.py:471
  38.0 1.7 %collective-permute-start.17 = (f32[49,8,128]{2,1,0:T(8,128)S(1)}, f32[49,8,128]{2,1,0:T(8,128)S(1)}, u32[]{:S(2)}, u32[]{:S(2)}) collective-permute-start(f32[49,8,128]{2,1,0:T(8,128)S(1)} %collective-permute-done.16.refs_7_), channel_id=1, source_target_pairs={{0,1},{1,0},{2,3},{3,2},{4,5},{5,4},{6,7},{7,6},{8,9},{9,8},{10,11... | collective-permute-start | bytes 602120 | tf_op jit(solution)/shard_map/ppermute | solution.py:471
  74.9 1.7 %collective-permute-start.33 = (f32[96,512]{1,0:T(8,128)}, f32[96,512]{1,0:T(8,128)S(1)}, u32[]{:S(2)}, u32[]{:S(2)}) collective-permute-start(f32[96,512]{1,0:T(8,128)} %get-tuple-element.262), channel_id=1, source_target_pairs={{0,1},{1,0},{2,3},{3,2},{4,5},{5,4},{6,7},{7,6},{8,9},{9,8},{10,11... | collective-permute-start | bytes 589832 | tf_op jit(solution)/shard_map/ppermute | solution.py:471
  75.2 2.7 %collective-permute-start.31 = (f32[96,512]{1,0:T(8,128)}, f32[96,512]{1,0:T(8,128)S(1)}, u32[]{:S(2)}, u32[]{:S(2)}) collective-permute-start(f32[96,512]{1,0:T(8,128)} %get-tuple-element.260), channel_id=1, source_target_pairs={{0,1},{1,0},{2,3},{3,2},{4,5},{5,4},{6,7},{7,6},{8,9},{9,8},{10,11... | collective-permute-start | bytes 589832 | tf_op jit(solution)/shard_map/ppermute | solution.py:471
  75.5 2.7 %collective-permute-start.29 = (f32[96,512]{1,0:T(8,128)}, f32[96,512]{1,0:T(8,128)S(1)}, u32[]{:S(2)}, u32[]{:S(2)}) collective-permute-start(f32[96,512]{1,0:T(8,128)} %get-tuple-element.258), channel_id=1, source_target_pairs={{0,1},{1,0},{2,3},{3,2},{4,5},{5,4},{6,7},{7,6},{8,9},{9,8},{10,11... | collective-permute-start | bytes 589832 | tf_op jit(solution)/shard_map/ppermute | solution.py:471
  75.7 2.8 %collective-permute-start.23 = (f32[96,512]{1,0:T(8,128)}, f32[96,512]{1,0:T(8,128)S(1)}, u32[]{:S(2)}, u32[]{:S(2)}) collective-permute-start(f32[96,512]{1,0:T(8,128)} %get-tuple-element.246), channel_id=1, source_target_pairs={{0,1},{1,0},{2,3},{3,2},{4,5},{5,4},{6,7},{7,6},{8,9},{9,8},{10,11... | collective-permute-start | bytes 589832 | tf_op jit(solution)/shard_map/ppermute | solution.py:471
  76.0 4.1 %collective-permute-start.21 = (f32[96,512]{1,0:T(8,128)}, f32[96,512]{1,0:T(8,128)S(1)}, u32[]{:S(2)}, u32[]{:S(2)}) collective-permute-start(f32[96,512]{1,0:T(8,128)} %get-tuple-element.244), channel_id=1, source_target_pairs={{0,1},{1,0},{2,3},{3,2},{4,5},{5,4},{6,7},{7,6},{8,9},{9,8},{10,11... | collective-permute-start | bytes 589832 | tf_op jit(solution)/shard_map/ppermute | solution.py:471
  76.6 4.8 %collective-permute-start.19 = (f32[96,512]{1,0:T(8,128)}, f32[96,512]{1,0:T(8,128)S(1)}, u32[]{:S(2)}, u32[]{:S(2)}) collective-permute-start(f32[96,512]{1,0:T(8,128)} %get-tuple-element.242), channel_id=1, source_target_pairs={{0,1},{1,0},{2,3},{3,2},{4,5},{5,4},{6,7},{7,6},{8,9},{9,8},{10,11... | collective-permute-start | bytes 589832 | tf_op jit(solution)/shard_map/ppermute | solution.py:471
  76.8 3.2 %copy-start.13 = (f32[96,512]{1,0:T(8,128)S(1)}, f32[96,512]{1,0:T(8,128)}, u32[]{:S(2)}) copy-start(f32[96,512]{1,0:T(8,128)} %get-tuple-element.259) | copy-start | bytes 589828
  77.9 6.4 %collective-permute-start.35 = (f32[96,512]{1,0:T(8,128)}, f32[96,512]{1,0:T(8,128)S(1)}, u32[]{:S(2)}, u32[]{:S(2)}) collective-permute-start(f32[96,512]{1,0:T(8,128)} %get-tuple-element.269), channel_id=1, source_target_pairs={{0,1},{1,0},{2,3},{3,2},{4,5},{5,4},{6,7},{7,6},{8,9},{9,8},{10,11... | collective-permute-start | bytes 589832 | tf_op jit(solution)/shard_map/ppermute | solution.py:471
  78.2 7.7 %collective-permute-start.25 = (f32[96,512]{1,0:T(8,128)S(1)}, f32[96,512]{1,0:T(8,128)S(1)}, u32[]{:S(2)}, u32[]{:S(2)}) collective-permute-start(f32[96,512]{1,0:T(8,128)S(1)} %copy-done.28), channel_id=1, source_target_pairs={{0,1},{1,0},{2,3},{3,2},{4,5},{5,4},{6,7},{7,6},{8,9},{9,8},{10,11... | collective-permute-start | bytes 589832 | tf_op jit(solution)/shard_map/ppermute | solution.py:471
  78.4 8.7 %collective-permute-start.34 = (f32[96,512]{1,0:T(8,128)S(1)}, f32[96,512]{1,0:T(8,128)S(1)}, u32[]{:S(2)}, u32[]{:S(2)}) collective-permute-start(f32[96,512]{1,0:T(8,128)S(1)} %add.180), channel_id=1, source_target_pairs={{0,6},{1,7},{2,4},{3,5},{4,2},{5,3},{6,0},{7,1},{8,14},{9,15},{10,... | collective-permute-start | bytes 589832 | tf_op jit(solution)/shard_map/ppermute | solution.py:471
  80.1 15.5 %collective-permute-start.32 = (f32[96,512]{1,0:T(8,128)S(1)}, f32[96,512]{1,0:T(8,128)S(1)}, u32[]{:S(2)}, u32[]{:S(2)}) collective-permute-start(f32[96,512]{1,0:T(8,128)S(1)} %add.179), channel_id=1, source_target_pairs={{0,4},{1,5},{2,6},{3,7},{4,0},{5,1},{6,2},{7,3},{8,12},{9,13},{10,... | collective-permute-start | bytes 589832 | tf_op jit(solution)/shard_map/ppermute | solution.py:471
  81.5 14.1 %collective-permute-start.30 = (f32[96,512]{1,0:T(8,128)S(1)}, f32[96,512]{1,0:T(8,128)S(1)}, u32[]{:S(2)}, u32[]{:S(2)}) collective-permute-start(f32[96,512]{1,0:T(8,128)S(1)} %add.178), channel_id=1, source_target_pairs={{0,2},{1,3},{2,0},{3,1},{4,6},{5,7},{6,4},{7,5},{8,10},{9,11},{10,... | collective-permute-start | bytes 589832 | tf_op jit(solution)/shard_map/ppermute | solution.py:471
  84.3 10.3 %copy-start.8 = (f32[96,512]{1,0:T(8,128)S(1)}, f32[96,512]{1,0:T(8,128)}, u32[]{:S(2)}) copy-start(f32[96,512]{1,0:T(8,128)} %get-tuple-element.268) | copy-start | bytes 589828
  84.3 15.6 %collective-permute-start.24 = (f32[96,512]{1,0:T(8,128)S(1)}, f32[96,512]{1,0:T(8,128)S(1)}, u32[]{:S(2)}, u32[]{:S(2)}) collective-permute-start(f32[96,512]{1,0:T(8,128)S(1)} %add.164), channel_id=1, source_target_pairs={{0,6},{1,7},{2,4},{3,5},{4,2},{5,3},{6,0},{7,1},{8,14},{9,15},{10,... | collective-permute-start | bytes 589832 | tf_op jit(solution)/shard_map/ppermute | solution.py:471
  85.9 14.0 %collective-permute-start.22 = (f32[96,512]{1,0:T(8,128)S(1)}, f32[96,512]{1,0:T(8,128)S(1)}, u32[]{:S(2)}, u32[]{:S(2)}) collective-permute-start(f32[96,512]{1,0:T(8,128)S(1)} %add.163), channel_id=1, source_target_pairs={{0,4},{1,5},{2,6},{3,7},{4,0},{5,1},{6,2},{7,3},{8,12},{9,13},{10,... | collective-permute-start | bytes 589832 | tf_op jit(solution)/shard_map/ppermute | solution.py:471
  87.2 12.8 %collective-permute-start.20 = (f32[96,512]{1,0:T(8,128)S(1)}, f32[96,512]{1,0:T(8,128)S(1)}, u32[]{:S(2)}, u32[]{:S(2)}) collective-permute-start(f32[96,512]{1,0:T(8,128)S(1)} %add.162), channel_id=1, source_target_pairs={{0,2},{1,3},{2,0},{3,1},{4,6},{5,7},{6,4},{7,5},{8,10},{9,11},{10,... | collective-permute-start | bytes 589832 | tf_op jit(solution)/shard_map/ppermute | solution.py:471
  89.3 12.6 %all-to-all-start = ((f32[32,1,320]{2,1,0:T(1,128)}), f32[32,1,320]{2,1,0:T(1,128)S(1)}, u32[]{:S(2)}, u32[]{:S(2)}) async-start(f32[32,1,320]{2,1,0:T(1,128)} %pad_maximum_fusion), calls=%async_computation | async-start | bytes 98304 | tf_op jit(solution)/shard_map/all_to_all | solution.py:575
  95.7 9.0 %collective-permute-start.37 = (f32[32,512]{1,0:T(8,128)S(1)}, f32[32,512]{1,0:T(8,128)S(1)}, u32[]{:S(2)}, u32[]{:S(2)}) collective-permute-start(f32[32,512]{1,0:T(8,128)S(1)} %get-tuple-element.309), channel_id=1, source_target_pairs={{0,16},{1,17},{2,18},{3,19},{4,20},{5,21},{6,22},{7,23},{8,24},{9,... | collective-permute-start | bytes 196616 | tf_op jit(solution)/shard_map/ppermute | solution.py:610
  98.4 8.3 %collective-permute-start.38 = (f32[32,512]{1,0:T(8,128)S(1)}, f32[32,512]{1,0:T(8,128)S(1)}, u32[]{:S(2)}, u32[]{:S(2)}) collective-permute-start(f32[32,512]{1,0:T(8,128)S(1)} %get-tuple-element.308), channel_id=1, source_target_pairs={{0,24},{1,25},{2,26},{3,27},{4,28},{5,29},{6,30},{7,31},{8,16},{9,... | collective-permute-start | bytes 196616 | tf_op jit(solution)/shard_map/ppermute | solution.py:610
  99.9 6.8 %collective-permute-start.36 = (f32[32,512]{1,0:T(8,128)S(1)}, f32[32,512]{1,0:T(8,128)S(1)}, u32[]{:S(2)}, u32[]{:S(2)}) collective-permute-start(f32[32,512]{1,0:T(8,128)S(1)} %get-tuple-element.310), channel_id=1, source_target_pairs={{0,8},{1,9},{2,10},{3,11},{4,12},{5,13},{6,14},{7,15},{8,0},{9,1},... | collective-permute-start | bytes 196616 | tf_op jit(solution)/shard_map/ppermute | solution.py:610
  102.0 4.5 %copy-start.19 = (f32[16,512]{1,0:T(8,128)S(1)}, f32[16,512]{1,0:T(8,128)}, u32[]{:S(2)}) copy-start(f32[16,512]{1,0:T(8,128)} %get-tuple-element.291) | copy-start | bytes 98308
  102.0 6.7 %collective-permute-start.28 = (f32[32,512]{1,0:T(8,128)S(1)}, f32[32,512]{1,0:T(8,128)S(1)}, u32[]{:S(2)}, u32[]{:S(2)}) collective-permute-start(f32[32,512]{1,0:T(8,128)S(1)} %get-tuple-element.304), channel_id=1, source_target_pairs={{0,24},{1,25},{2,26},{3,27},{4,28},{5,29},{6,30},{7,31},{8,16},{9,... | collective-permute-start | bytes 196616 | tf_op jit(solution)/shard_map/ppermute | solution.py:610
  103.7 7.4 %collective-permute-start.27 = (f32[32,512]{1,0:T(8,128)S(1)}, f32[32,512]{1,0:T(8,128)S(1)}, u32[]{:S(2)}, u32[]{:S(2)}) collective-permute-start(f32[32,512]{1,0:T(8,128)S(1)} %get-tuple-element.305), channel_id=1, source_target_pairs={{0,16},{1,17},{2,18},{3,19},{4,20},{5,21},{6,22},{7,23},{8,24},{9,... | collective-permute-start | bytes 196616 | tf_op jit(solution)/shard_map/ppermute | solution.py:610
  104.7 6.5 %collective-permute-start.26 = (f32[32,512]{1,0:T(8,128)S(1)}, f32[32,512]{1,0:T(8,128)S(1)}, u32[]{:S(2)}, u32[]{:S(2)}) collective-permute-start(f32[32,512]{1,0:T(8,128)S(1)} %get-tuple-element.306), channel_id=1, source_target_pairs={{0,8},{1,9},{2,10},{3,11},{4,12},{5,13},{6,14},{7,15},{8,0},{9,1},... | collective-permute-start | bytes 196616 | tf_op jit(solution)/shard_map/ppermute | solution.py:610
  106.5 18.0 %copy-start.6 = (f32[192]{0:T(256)S(1)}, f32[192]{0:T(256)}, u32[]{:S(2)}) copy-start(f32[192]{0:T(256)} %param.21) | copy-start | bytes 2308
  106.7 4.5 %copy-start.3 = (s32[2,512]{1,0:T(2,128)S(1)}, s32[2,512]{1,0:T(2,128)}, u32[]{:S(2)}) copy-start(s32[2,512]{1,0:T(2,128)} %mask_ref.1) | copy-start | bytes 12292
  111.1 13.3 %copy-start.1 = (f32[64,512]{1,0:T(8,128)S(1)}, f32[64,512]{1,0:T(8,128)}, u32[]{:S(2)}) copy-start(f32[64,512]{1,0:T(8,128)} %refs_2_.1) | copy-start | bytes 393220
  111.1 13.3 %copy-start.2 = (f32[64,512]{1,0:T(8,128)S(1)}, f32[64,512]{1,0:T(8,128)}, u32[]{:S(2)}) copy-start(f32[64,512]{1,0:T(8,128)} %refs_3_.1) | copy-start | bytes 393220
  111.9 12.6 %copy-start = (f32[64,512]{1,0:T(8,128)S(1)}, f32[64,512]{1,0:T(8,128)}, u32[]{:S(2)}) copy-start(f32[64,512]{1,0:T(8,128)} %refs_1_.1) | copy-start | bytes 393220
  111.9 12.5 %all-to-all-start.1 = ((f32[32,1,256]{2,1,0:T(1,128)}), f32[32,1,256]{2,1,0:T(1,128)S(1)}, u32[]{:S(2)}, u32[]{:S(2)}) async-start(f32[32,1,256]{2,1,0:T(1,128)} %get-tuple-element.290), calls=%async_computation.1 | async-start | bytes 65536 | tf_op jit(solution)/shard_map/all_to_all | solution.py:575
  (13 other events, 13.8 us)
